TPU v7x, 256 devices: a whole 4x4x8 slice. The times are simulated.
256 devices in a mesh: row: 16 (over x, y_lo, core), col: 16 (over y_hi, z).
Axes of the slice: x: 4, y: 4 (y_hi: 2, y_lo: 2; y = y_hi * 2 + y_lo), z: 8, core: 2. Of those that a mesh axis runs over, the one named last changes fastest.
Arguments:
- layer_input: bfloat16 [24576, 2048], P('col', 'row'), may hold values from -65 to 65
- grad_output: bfloat16 [24576, 8192], P('col', 'row'), may hold values from -0.41462717 to 0.41462717
- hid_state: float32 [8192], P('col'), may hold values from 2 to 40
- feat_state: float32 [2048], P('row'), may hold values from 2 to 40
Outputs:
- update: float32 [8192, 2048], P('col', 'row')
- hid_new: float32 [8192], P('col')
- feat_new: float32 [2048], P('row')
- update_rms: float32 [], replicated
All inputs are finite; a program needn't handle non-finite values.
Results may differ from a plain program's by a relative error of at most 0.0003.
Values may be sent and summed in bfloat16 or wider, within the bound.
A program may use at most 128 MiB of HBM per device.

v0:
```python
import jax
import jax.numpy as jnp
from jax import lax
from jax.sharding import PartitionSpec as P

decay_rate = 0.8415106807538887


def contract_tokens(left, right):
    return lax.dot_general(
        left, right, (((0,), (0,)), ((), ())), preferred_element_type=jnp.float32
    )


def body(layer_input, grad_output, hid_state, feat_state):
    rows_here = hid_state.shape[0]
    feat_here = feat_state.shape[0]
    hid_count = rows_here * lax.axis_size("col")
    feat_count = feat_here * lax.axis_size("row")
    full_output = lax.all_gather(grad_output, "row", axis=1, tiled=True)
    grad = lax.psum_scatter(
        contract_tokens(full_output, layer_input), "col", scatter_dimension=0, tiled=True
    )
    squares = grad * grad + 1e-30
    local_hid = jnp.sum(squares, axis=1)
    local_feat = jnp.sum(squares, axis=0)
    hid_sum = lax.psum(local_hid, "row")
    feat_sum = lax.psum(local_feat, "col")
    hid_new = decay_rate * hid_state + (1.0 - decay_rate) * (hid_sum / feat_count)
    feat_new = decay_rate * feat_state + (1.0 - decay_rate) * (feat_sum / hid_count)
    hid_mean = lax.psum(jnp.sum(hid_new), "col") / hid_count
    raw = grad * jnp.sqrt(hid_mean / (hid_new[:, None] * feat_new[None, :]))
    total = lax.psum(jnp.sum(raw * raw), ("row", "col"))
    update_rms = jnp.sqrt(total / (hid_count * feat_count))
    update = raw / jnp.maximum(1.0, update_rms)
    return (update, hid_new, feat_new, update_rms)


def solution(mesh):
    in_specs = (P("col", "row"), P("col", "row"), P("col"), P("row"))
    out_specs = (P("col", "row"), P("col"), P("row"), P())
    return jax.shard_map(body, mesh=mesh, in_specs=in_specs, out_specs=out_specs, check_vma=False)
```

profile of v0, /device:TPU:1, one launch (start us, length us, event | category | flops | bytes accessed | tf_op | source)
XLA Modules:
  0.0 526.8 jit_solution(14945441488350949268)
XLA Ops:
  7.2 0.0 copy-start
  7.2 0.0 copy-start.3
  7.2 0.0 copy-start.4
  7.2 0.0 all-gather.2.cloned.1.call-start
  7.2 0.7 all-gather.2.cloned.1.call-update
  7.9 0.0 reduce-scatter.2.cloned.1.call-start
  8.0 139.7 %all-gather.2.cloned.1.call-done = bf16[1536,8192]{1,0:T(8,128)(2,1)} async-done(((bf16[1536,512]{1,0:T(8,128)(2,1)}), bf16[1536,8192]{1,0:T(8,128)(2,1)}) %all-gather.2.cloned.1.call-update) | async-done | bytes 25165840 | tf_op jit(solution)/shard_map/all_gather | solution.py:20
  147.7 0.0 copy-done
  147.7 13.6 %fusion.3 = f32[8192,128]{1,0:T(8,128)} fusion(bf16[1536,8192]{1,0:T(8,128)(2,1)} %all-gather.2.cloned.1.call-done, bf16[1536,128]{1,0:T(8,128)(2,1)S(1)} %copy-done), kind=kOutput, calls=%fused_computation.9 | convolution fusion | flops 3221225472 | bytes 29753344 | tf_op jit(solution)/shard_map/dot_general | solution.py:10
  161.3 0.0 reduce-scatter.2.cloned.1.call-update
  161.4 208.7 %reduce-scatter.2.cloned.1.call-done = f32[512,128]{1,0:T(8,128)} async-done(((f32[8192,128]{1,0:T(8,128)}), f32[512,128]{1,0:T(8,128)}) %reduce-scatter.2.cloned.1.call-update) | async-done | bytes 262160 | tf_op jit(solution)/shard_map/reduce_scatter | solution.py:21
  370.0 1.1 fusion.1
  371.1 31.7 %psum.28 = f32[512]{0:T(512)S(1)} all-reduce(f32[512]{0:T(512)S(1)} %get-tuple-element.4), channel_id=1, replica_groups=mesh['row'=16,'col'=16] {'row'}, use_global_device_ids=true, to_apply=%region_2.0 | all-reduce | flops 512 | bytes 4096 | tf_op jit(solution)/shard_map/psum | solution.py:27
  402.9 0.0 copy-done.3
  402.9 0.6 fusion.2
  403.5 0.0 copy-start.1
  403.5 32.4 %all-reduce = (f32[128]{0:T(128)S(1)}, f32[]{:T(128)}) all-reduce(f32[128]{0:T(128)S(1)} %get-tuple-element.5, f32[]{:T(128)} %get-tuple-element.8), channel_id=1, replica_groups=mesh['row'=16,'col'=16] {'col'}, use_global_device_ids=true, to_apply=%region_6.0 | all-reduce | flops 129 | bytes 1032 | tf_op jit(solution)/shard_map/psum | solution.py:28
  436.6 0.0 copy-done.4
  436.6 0.0 copy-start.2
  436.6 1.8 multiply_reduce_fusion
  438.3 77.9 %psum.31 = f32[]{:T(128)} all-reduce(f32[]{:T(128)} %multiply_reduce_fusion), channel_id=1, replica_groups=mesh['row'=16,'col'=16] {'row','col'}, use_global_device_ids=true, to_apply=%region_8.0 | all-reduce | flops 1 | bytes 8 | tf_op jit(solution)/shard_map/psum | solution.py:33
  517.0 1.8 broadcast_divide_fusion
  518.8 0.0 copy-done.1
  518.8 0.0 copy-done.2
  (1 shorter events, 0.0 us)
Async XLA Ops:
  7.2 140.6 %copy-start = (bf16[1536,128]{1,0:T(8,128)(2,1)S(1)}, bf16[1536,128]{1,0:T(8,128)(2,1)}, u32[]{:S(2)}) copy-start(bf16[1536,128]{1,0:T(8,128)(2,1)} %param.4) | copy-start | bytes 1179652
  7.2 395.7 %copy-start.3 = (f32[512]{0:T(512)S(1)}, f32[512]{0:T(512)}, u32[]{:S(2)}) copy-start(f32[512]{0:T(512)} %param.6) | copy-start | bytes 6148
  7.2 429.4 %copy-start.4 = (f32[128]{0:T(128)S(1)}, f32[128]{0:T(128)}, u32[]{:S(2)}) copy-start(f32[128]{0:T(128)} %param.7) | copy-start | bytes 1540
  7.2 140.5 %all-gather.2.cloned.1.call-start = ((), (), s32[]{:S(2)}) async-start(), calls=%async_computation.1 | async-start | bytes 26738688 | tf_op jit(solution)/shard_map/all_gather | solution.py:20
  7.9 362.1 %reduce-scatter.2.cloned.1.call-start = ((), (), s32[]{:S(2)}) async-start(), calls=%async_computation.2 | async-start | bytes 4456448 | tf_op jit(solution)/shard_map/reduce_scatter | solution.py:21
  403.5 115.3 %copy-start.1 = (f32[512]{0:T(512)}, f32[512]{0:T(512)S(1)}, u32[]{:S(2)}) copy-start(f32[512]{0:T(512)S(1)} %get-tuple-element.9) | copy-start | bytes 6148
  436.6 82.2 %copy-start.2 = (f32[128]{0:T(128)}, f32[128]{0:T(128)S(1)}, u32[]{:S(2)}) copy-start(f32[128]{0:T(128)S(1)} %multiply_add_fusion.2) | copy-start | bytes 1540
Sparse Core Ops, SparseCore 0:
  9.8 137.8 all-gather.1
  161.5 208.5 reduce-scatter.1
where the time goes:
time: 527 us
  waiting for transfers between devices  349 us (66%)
  blocking collectives  142 us (27%)
  between operations  16.6 us (3%)
  matrix products  13.6 us (3%)
  other arithmetic  5.3 us (1%)
    reduce_scatter x1, waiting for transfers between devices, body(): lax.psum_scatter(contract_tokens(full_output, layer_input), 'col', scatte...  209 us
    all_gather x1, waiting for transfers between devices, body(): full_output = lax.all_gather(grad_output, 'row', axis=1, tiled=True)  140 us
    psum x1, blocking collectives, body(): total = lax.psum(jnp.sum(raw * raw), ('row', 'col'))  77.9 us
    psum x1, blocking collectives, body(): feat_sum = lax.psum(local_feat, 'col')  32.4 us
    psum x1, blocking collectives, body(): hid_sum = lax.psum(local_hid, 'row')  31.7 us
    dot_general x1, matrix products, contract_tokens(): lax.dot_general(left, right, (((0,), (0,)), ((), ())), preferred_element_...  13.6 us
  transfers between devices with their start and end apart: 2, of which 2 were waited for; matrix products, arithmetic and copies ran while one was open for 0% of the time, Pallas kernels for 0%

commit v1 on v0

v1 whole, which is shorter than its diff:
```python
import functools
import jax
import jax.numpy as jnp
from jax import lax
from jax.sharding import PartitionSpec as P
from jax.experimental import pallas as pl
from jax.experimental.pallas import tpu as pltpu

decay_rate = 0.8415106807538887
MESH = pl.DeviceIdType.MESH
PAIRS = 8
MSG = jnp.float32


def rem(a, n):
    return lax.rem(a, n)


def kernel(
    tokens, hid_count, feat_count,
    x_hbm, g_hbm, hs_ref, fs_ref,
    upd_ref, hid_ref, feat_ref, rms_ref,
    gv, gt, xp, pb, sb, rb, fin, yr, ga, ar, tile, racc, hsend, hr, hb, cs, cr, ts, tr,
    lsem, gsend, grecv, crecv, ssem, rsem, ysend, yrecv, asend, arecv, bsend, brecv,
    hsem, hrecv, hbsend, hbrecv, csend, csrecv, tsend, trecv,
):
    r = lax.axis_index("row")
    c = lax.axis_index("col")
    x, yl, k = r // 4, rem(r // 2, 2), rem(r, 2)
    yh, z = c // 8, rem(c, 8)
    part = 2 * z + yh

    def row_of(dx, dy, kk):
        return rem(x + dx, 4) * 4 + rem(yl + dy, 2) * 2 + kk

    def remote(src, dst, send, recv, dev):
        return pltpu.make_async_remote_copy(
            src_ref=src, dst_ref=dst, send_sem=send, recv_sem=recv,
            device_id=dev, device_id_type=MESH,
        )

    lanes = pl.ds(pl.multiple_of(k * 128, 128), 128)
    other_lanes = pl.ds(pl.multiple_of((1 - k) * 128, 128), 128)
    copy_x = pltpu.make_async_copy(x_hbm, xp.at[0, :, lanes], lsem.at[0])
    copy_x.start()
    copy_g = pltpu.make_async_copy(g_hbm, gv, lsem.at[1])
    copy_g.start()

    barrier = pltpu.get_barrier_semaphore()
    for i in range(1, 16):
        pl.semaphore_signal(barrier, inc=1, device_id=(rem(r + i, 16), c), device_id_type=MESH)
        pl.semaphore_signal(barrier, inc=1, device_id=(r, rem(c + i, 16)), device_id_type=MESH)
    copy_x.wait()
    pl.semaphore_wait(barrier, 30)

    east = (row_of(1, 0, k), c)
    west = (row_of(3, 0, k), c)
    side = (row_of(0, 1, k), c)
    mate = (row_of(0, 0, 1 - k), c)
    half = tokens // 2
    whole, low, high = pl.ds(0, tokens), pl.ds(0, half), pl.ds(half, half)

    def send_block(src_slot, dst_slot, rows, send, recv, dev):
        return remote(xp.at[src_slot, rows, lanes], xp.at[dst_slot, rows, lanes], gsend.at[send], grecv.at[recv], dev)

    def mate_copy(slot):
        return remote(xp.at[slot, :, lanes], xp.at[slot, :, lanes], gsend.at[8 + slot], crecv.at[slot], mate)

    sends = {
        "e0": send_block(0, 3, whole, 0, 3, east),
        "w0": send_block(0, 2, whole, 1, 2, west),
        "s0": send_block(0, 1, whole, 2, 1, side),
        "e1": send_block(1, 6, whole, 3, 6, east),
        "w1": send_block(1, 5, whole, 4, 5, west),
        "e3": send_block(3, 4, low, 5, 4, east),
        "w2": send_block(2, 4, high, 6, 0, west),
        "s4": send_block(4, 7, whole, 7, 7, side),
    }

    def wait_block(slot):
        if slot == 4:
            send_block(4, 4, low, 0, 4, east).wait_recv()
            send_block(4, 4, high, 0, 0, east).wait_recv()
        else:
            send_block(slot, slot, whole, 0, slot, east).wait_recv()

    def wait_mate(slot):
        remote(xp.at[slot, :, other_lanes], xp.at[slot, :, other_lanes], gsend.at[0], crecv.at[slot], mate).wait_recv()

    for name in ("e0", "w0", "s0"):
        sends[name].start()
    mate_copy(0).start()
    copy_g.wait()
    gt[...] = gv[...].T
    racc[...] = jnp.zeros_like(racc)

    def message(s, m, sign):
        dev = (r, yh * 8 + rem(z + sign + 8, 8))
        return remote(sb.at[s, m], rb.at[s, m], ssem.at[s, m], rsem.at[s, m], dev)

    def chunk(s, offset):
        rows = pl.ds(pl.multiple_of(rem(z + offset + 8, 8) * 64, 64), 64)
        return pb[s, rows, :]

    def index(d, sign):
        return 0 if d == 4 else 7 - 2 * d + (0 if sign > 0 else 1)

    def push(s, m, sign, value):
        sb[s, m] = value.astype(MSG)
        message(s, m, sign).start()

    def got(s, m):
        message(s, m, 1).wait_recv()
        return rb[s, m].astype(jnp.float32)

    def slot_offset(p):
        dy = jnp.where(jnp.logical_or(p == 1, p >= 5), 1, 0)
        one = jnp.logical_or(p == 2, p == 5)
        three = jnp.logical_or(p == 3, p == 6)
        two = jnp.logical_or(p == 4, p == 7)
        dx = jnp.where(one, 1, 0) + jnp.where(two, 2, 0) + jnp.where(three, 3, 0)
        return dx, dy

    y_mate = (r, (1 - yh) * 8 + z)

    def y_copy(s):
        rows = pl.ds(pl.multiple_of((1 - yh) * 32, 32), 32)
        return remote(fin.at[s, rows], yr.at[s], ysend.at[s], yrecv.at[s], y_mate)

    def a_copy(s, kk, f):
        return remote(ga.at[s, kk], ar.at[r], asend.at[s, kk], arecv.at[r], (f, c))

    def within(s):
        return jnp.logical_and(s >= 0, s < PAIRS)

    def step(t, carry):
        for d in (1, 2):
            s = t - 4 + d

            @pl.when(within(s))
            def _():
                for sign in (1, -1):
                    push(s, index(d, sign), sign, chunk(s, sign * d) + got(s, index(d + 1, sign)))

        s3 = t - 1

        @pl.when(within(s3))
        def _():
            par = rem(s3, 2)
            for sign in (1, -1):
                long = par == (0 if sign > 0 else 1)

                @pl.when(long)
                def _():
                    push(s3, index(3, sign), sign, chunk(s3, sign * 3) + got(s3, 0))

                @pl.when(jnp.logical_not(long))
                def _():
                    push(s3, index(3, sign), sign, chunk(s3, sign * 3))

        @pl.when(t == 1)
        def _():
            wait_block(1)
            mate_copy(1).start()
            wait_block(3)
            sends["e3"].start()
            mate_copy(3).start()
            wait_block(2)
            sends["w2"].start()
            mate_copy(2).start()
            sends["e1"].start()
            sends["w1"].start()

        @pl.when(t == 3)
        def _():
            wait_block(4)
            sends["s4"].start()
            mate_copy(4).start()

        for slot in (5, 6, 7):
            @pl.when(t == slot)
            def _():
                wait_block(slot)
                mate_copy(slot).start()

        @pl.when(t < PAIRS)
        def _():
            wait_mate_dyn(t)
            pb[t] = jnp.dot(gt[...], xp[t], preferred_element_type=jnp.float32)
            sign = 1 - 2 * rem(t, 2)
            push(t, 0, sign, chunk(t, 4))

        s0 = t - 4

        @pl.when(within(s0))
        def _():
            fin[s0] = chunk(s0, 0) + got(s0, 5) + got(s0, 6)
            y_copy(s0).start()

        sy = t - 5

        @pl.when(within(sy))
        def _():
            y_copy(sy).wait_recv()
            rows = pl.ds(pl.multiple_of(yh * 32, 32), 32)
            g = fin[sy, rows, :] + yr[sy]
            racc[...] += g * g + 1e-30
            dx, dy = slot_offset(sy)
            for kk in (0, 1):
                ga[sy, kk] = g[:, kk * 128:(kk + 1) * 128]
                f = row_of(dx, dy, kk)
                here = jnp.logical_and(sy == 0, k == kk)

                @pl.when(here)
                def _():
                    ar[r] = g[:, kk * 128:(kk + 1) * 128]

                @pl.when(jnp.logical_not(here))
                def _():
                    a_copy(sy, kk, f).start()

        return carry

    def wait_mate_dyn(t):
        remote(xp.at[t, :, other_lanes], xp.at[t, :, other_lanes], gsend.at[0], crecv.at[t], mate).wait_recv()

    lax.fori_loop(0, PAIRS + 5, step, 0)

    sums = jnp.sum(racc[...], axis=1, keepdims=True)
    lane = lax.broadcasted_iota(jnp.int32, (32, 128), 1)
    line = lax.broadcasted_iota(jnp.int32, (32, 128), 0)
    placed = jnp.sum(jnp.where(lane == line + rem(part, 4) * 32, sums, 0.0), axis=0, keepdims=True)
    diagonal = r == c
    h_copy = remote(hsend, hr.at[part], hsem, hrecv.at[part], (r, r))

    @pl.when(diagonal)
    def _():
        hr[part] = placed

    @pl.when(jnp.logical_not(diagonal))
    def _():
        hsend[...] = placed
        h_copy.start()

    def b_copy(q):
        return remote(ar.at[q], tile.at[part], bsend.at[q], brecv.at[part], (r, q))

    def wait_a(q):
        remote(ar.at[q], ar.at[q], asend.at[0, 0], arecv.at[q], mate).wait_recv()

    def b_step(i, carry):
        q = rem(c + i, 16)

        @pl.when(q != r)
        def _():
            wait_a(q)

        @pl.when(i == 0)
        def _():
            tile[part] = ar[c]

        @pl.when(i > 0)
        def _():
            b_copy(q).start()

        return carry

    lax.fori_loop(0, 16, b_step, 0)

    def hb_copy(i):
        return remote(hb, hb, hbsend.at[i], hbrecv, (rem(r + i, 16), c))

    @pl.when(diagonal)
    def _():
        def wait_h(i, carry):
            q = rem(part + i, 16)
            remote(hr.at[q], hr.at[q], hsem, hrecv.at[q], mate).wait_recv()
            return carry

        lax.fori_loop(1, 16, wait_h, 0)
        for q in range(4):
            total = hr[4 * q] + hr[4 * q + 1] + hr[4 * q + 2] + hr[4 * q + 3]
            hb[q:q + 1, :] = decay_rate * hs_ref[q:q + 1, :] + (1.0 - decay_rate) * (total / feat_count)

        for i in range(1, 16):
            hb_copy(i).start()

    @pl.when(jnp.logical_not(diagonal))
    def _():
        hb_copy(1).wait_recv()

    hid_ref[...] = hb[...]
    eye = lax.broadcasted_iota(jnp.int32, (128, 128), 0) == lax.broadcasted_iota(jnp.int32, (128, 128), 1)
    columns = [jnp.sum(jnp.where(eye, hb[q:q + 1, :], 0.0), axis=1, keepdims=True) for q in range(4)]

    def wait_b(i, carry):
        q = rem(part + i, 16)
        remote(tile.at[q], tile.at[q], bsend.at[0], brecv.at[q], mate).wait_recv()
        return carry

    lax.fori_loop(1, 16, wait_b, 0)
    fsum = jnp.zeros((1, 128), jnp.float32)
    wsum = jnp.zeros((1, 128), jnp.float32)
    for q in range(4):
        g = tile[4 * q:4 * q + 4].reshape(128, 128)
        sq = g * g
        fsum += jnp.sum(sq + 1e-30, axis=0, keepdims=True)
        wsum += jnp.sum(sq / columns[q], axis=0, keepdims=True)
    cr[c, 0:1, :] = fsum
    cr[c, 1:2, :] = wsum
    cr[c, 2:3, :] = jnp.full((1, 128), jnp.sum(hb[...]), jnp.float32)
    cr[c, 3:8, :] = jnp.zeros((5, 128), jnp.float32)

    def c_copy(i):
        return remote(cr.at[c], cr.at[c], csend.at[i], csrecv.at[c], (r, rem(c + i, 16)))

    for i in range(1, 16):
        c_copy(i).start()

    def wait_c(i, carry):
        q = rem(c + i, 16)
        remote(cr.at[q], cr.at[q], csend.at[0], csrecv.at[q], mate).wait_recv()
        return carry

    lax.fori_loop(1, 16, wait_c, 0)
    both = jnp.sum(cr[...], axis=0)
    feat = decay_rate * fs_ref[...] + (1.0 - decay_rate) * (both[0:1, :] / hid_count)
    feat_ref[...] = feat
    hid_mean = both[2:3, :] / hid_count
    tr[r] = jnp.full((1, 128), jnp.sum(both[1:2, :] / feat), jnp.float32)

    def t_copy(i):
        return remote(tr.at[r], tr.at[r], tsend.at[i], trecv.at[r], (rem(r + i, 16), c))

    for i in range(1, 16):
        t_copy(i).start()

    def drain(s, carry):
        for m in range(7):
            message(s, m, 1).wait_send()
        y_copy(s).wait_send()
        for kk in (0, 1):
            @pl.when(jnp.logical_not(jnp.logical_and(s == 0, k == kk)))
            def _():
                a_copy(s, kk, r).wait_send()
        mate_copy(s).wait_send()
        return carry

    lax.fori_loop(0, PAIRS, drain, 0)
    for one in sends.values():
        one.wait_send()

    def drain_b(i, carry):
        b_copy(rem(c + i, 16)).wait_send()
        c_copy(i).wait_send()
        return carry

    lax.fori_loop(1, 16, drain_b, 0)

    @pl.when(jnp.logical_not(diagonal))
    def _():
        h_copy.wait_send()

    @pl.when(diagonal)
    def _():
        for i in range(1, 16):
            hb_copy(i).wait_send()

    def wait_t(i, carry):
        q = rem(r + i, 16)
        remote(tr.at[q], tr.at[q], tsend.at[0], trecv.at[q], mate).wait_recv()
        t_copy(i).wait_send()
        return carry

    lax.fori_loop(1, 16, wait_t, 0)
    mean = hid_mean * jnp.sum(tr[...], axis=0) / (hid_count * feat_count)
    rms = jnp.sqrt(mean)
    rms_ref[...] = rms
    across = jnp.sqrt(hid_mean / feat) / jnp.maximum(1.0, rms)
    for q in range(4):
        g = tile[4 * q:4 * q + 4].reshape(128, 128)
        upd_ref[128 * q:128 * q + 128, :] = g * lax.rsqrt(columns[q]) * across


def body(layer_input, grad_output, hid_state, feat_state):
    tokens = layer_input.shape[0]
    hid_count, feat_count = 8192.0, 2048.0
    vm = pl.BlockSpec(memory_space=pltpu.VMEM)
    hbm = pl.BlockSpec(memory_space=pl.ANY)
    f32, bf16 = jnp.float32, jnp.bfloat16
    dma = pltpu.SemaphoreType.DMA
    update, hid, feat, rms = pl.pallas_call(
        functools.partial(kernel, tokens, hid_count, feat_count),
        name="optimizer_step",
        out_shape=(
            jax.ShapeDtypeStruct((512, 128), f32),
            jax.ShapeDtypeStruct((4, 128), f32),
            jax.ShapeDtypeStruct((1, 128), f32),
            jax.ShapeDtypeStruct((1, 128), f32),
        ),
        in_specs=[hbm, hbm, vm, vm],
        out_specs=(vm, vm, vm, vm),
        scratch_shapes=[
            pltpu.VMEM((tokens, 512), bf16),
            pltpu.VMEM((512, tokens), bf16),
            pltpu.VMEM((PAIRS, tokens, 256), bf16),
            pltpu.VMEM((PAIRS, 512, 256), f32),
            pltpu.VMEM((PAIRS, 7, 64, 256), MSG),
            pltpu.VMEM((PAIRS, 7, 64, 256), MSG),
            pltpu.VMEM((PAIRS, 64, 256), f32),
            pltpu.VMEM((PAIRS, 32, 256), f32),
            pltpu.VMEM((PAIRS, 2, 32, 128), f32),
            pltpu.VMEM((16, 32, 128), f32),
            pltpu.VMEM((16, 32, 128), f32),
            pltpu.VMEM((32, 256), f32),
            pltpu.VMEM((1, 128), f32),
            pltpu.VMEM((16, 1, 128), f32),
            pltpu.VMEM((4, 128), f32),
            pltpu.VMEM((8, 128), f32),
            pltpu.VMEM((16, 8, 128), f32),
            pltpu.VMEM((1, 128), f32),
            pltpu.VMEM((16, 1, 128), f32),
            dma((2,)), dma((16,)), dma((8,)), dma((PAIRS,)),
            dma((PAIRS, 7)), dma((PAIRS, 7)), dma((PAIRS,)), dma((PAIRS,)),
            dma((PAIRS, 2)), dma((16,)), dma((16,)), dma((16,)),
            dma, dma((16,)), dma((16,)), dma,
            dma((16,)), dma((16,)), dma((16,)), dma((16,)),
        ],
        compiler_params=pltpu.CompilerParams(
            collective_id=0, has_side_effects=True, vmem_limit_bytes=50 << 20
        ),
    )(layer_input, grad_output, hid_state.reshape(4, 128), feat_state.reshape(1, 128))
    return update, hid.reshape(512), feat.reshape(128), rms[0, 0]


def solution(mesh):
    in_specs = (P("col", "row"), P("col", "row"), P("col"), P("row"))
    out_specs = (P("col", "row"), P("col"), P("row"), P())
    return jax.shard_map(body, mesh=mesh, in_specs=in_specs, out_specs=out_specs, check_vma=False)
```

time: 527 us -> 108 us (0.20)
  waiting for transfers between devices: 349 us -> 0 us
  blocking collectives: 142 us -> 0 us
  Pallas kernels: 0 us -> 100 us
  between operations: 16.6 us -> 1.82 us
  matrix products: 13.6 us -> 0 us
  local copies, waits for them, and re-layouts: 0.03 us -> 5.53 us
  other arithmetic: 5.3 us -> 0 us
    reduce_scatter x1 -> x0, waiting for transfers between devices: 209 us -> none  [body(): lax.psum_scatter(contract_tokens(full_output, layer_input), 'col', scatte...]
    psum x3 -> x0, blocking collectives: 142 us -> none  [the longest x1 77.9 us: body(): total = lax.psum(jnp.sum(raw * raw), ('row', 'col'))]
    all_gather x1 -> x0, waiting for transfers between devices: 140 us -> none  [body(): full_output = lax.all_gather(grad_output, 'row', axis=1, tiled=True)]
    pallas_call x0 -> x1, Pallas kernels: none -> 100 us  [body(): pl.pallas_call(functools.partial(kernel, tokens, hid_count, feat_count),...]
    dot_general x1 -> x0, matrix products: 13.6 us -> none  [contract_tokens(): lax.dot_general(left, right, (((0,), (0,)), ((), ())), preferred_element_...]
    unnamed x10 -> x11, local copies, waits for them, and re-layouts: 0.03 us -> 5.53 us
  transfers between devices with their start and end apart: 2 -> 0, of which waited for: 2 -> 0; matrix products, arithmetic and copies ran while one was open for 0% -> 0% of each run, Pallas kernels for 0% -> 0%
where the time goes in v1:
time: 108 us
  Pallas kernels  100 us (93%)
  local copies, waits for them, and re-layouts  5.53 us (5%)
  between operations  1.82 us (2%)
    pallas_call x1, Pallas kernels, body(): pl.pallas_call(functools.partial(kernel, tokens, hid_count, feat_count),...  100 us
    unnamed x11, local copies, waits for them, and re-layouts  5.53 us

profile of v1, /device:TPU:1, one launch (start us, length us, event | category | flops | bytes accessed | tf_op | source)
XLA Modules:
  0.0 107.6 jit_solution(4223736253277229166)
XLA Ops:
  0.6 0.0 copy-start
  0.6 1.4 %copy-done = bf16[1536,512]{1,0:T(8,128)(2,1)S(1)} copy-done((bf16[1536,512]{1,0:T(8,128)(2,1)S(1)}, bf16[1536,512]{1,0:T(8,128)(2,1)}, u32[]{:S(2)}) %copy-start) | copy-done | bytes 1572888
  2.0 0.0 copy-start.1
  2.0 1.0 copy-done.1
  3.0 0.0 copy-start.2
  3.0 0.7 copy-done.2
  3.7 0.0 copy-start.3
  3.7 0.7 copy-done.3
  4.4 100.2 %optimizer_step.1 = (f32[512,128]{1,0:T(8,128)S(1)}, f32[4,128]{1,0:T(4,128)S(1)}, f32[1,128]{1,0:T(1,128)S(1)}, f32[1,128]{1,0:T(1,128)S(1)}) custom-call(bf16[1536,128]{1,0:T(8,128)(2,1)S(1)} %copy-done.1, bf16[1536,512]{1,0:T(8,128)(2,1)S(1)} %copy-done, f32[4,128]{1,0:T(4,128)S(1)} %bitcast.6, f32[1,128]{1,0:T(1,128)S(1)} %bitcast.8), custom_call_target="tpu_custom_call" | custom-call | tf_op jit(solution)/shard_map/optimizer_step/pallas_call | solution.py:392
  104.6 0.7 copy.12
  105.3 0.6 copy.13
  105.9 0.5 copy.14
Async XLA Ops:
  0.6 1.4 %copy-start = (bf16[1536,512]{1,0:T(8,128)(2,1)S(1)}, bf16[1536,512]{1,0:T(8,128)(2,1)}, u32[]{:S(2)}) copy-start(bf16[1536,512]{1,0:T(8,128)(2,1)} %g_hbm.1) | copy-start | bytes 4718596
  2.0 1.0 copy-start.1
  3.0 0.7 copy-start.2
  3.7 0.7 copy-start.3

commit v2 on v1

v2 whole, which is shorter than its diff:
```python
import functools
import jax
import jax.numpy as jnp
from jax import lax
from jax.sharding import PartitionSpec as P
from jax.experimental import pallas as pl
from jax.experimental.pallas import tpu as pltpu

decay_rate = 0.8415106807538887
MESH = pl.DeviceIdType.MESH
PAIRS = 8
STEPS = 2 * PAIRS
MSG = jnp.bfloat16
POWER = 13
LIFT = 2.0 ** 9
TILE = 144
SPANS = ((2, 3, 2 * TILE, TILE), (4, 5, TILE, 2 * TILE), (6, 9, 0, 3 * TILE), (10, 11, 0, 2 * TILE), (12, 13, 0, TILE))


def rem(a, n):
    return lax.rem(a, n)


def encode(value):
    top = jnp.maximum(jnp.max(jnp.abs(value), axis=0, keepdims=True), 1e-30)
    scale = top.astype(MSG).astype(jnp.float32)
    m = value * (LIFT / scale)
    m2 = m * m
    m4 = m2 * m2
    coded = ((m * m4) * (m4 * m4)).astype(MSG)
    scales = [jnp.broadcast_to(scale[:, 128 * q:128 * q + 128], (8, 128)) for q in (0, 1)]
    return jnp.concatenate([coded[:, 0:128], coded[:, 128:256], jnp.concatenate(scales, axis=0).astype(MSG)], axis=0)


def decode(tile):
    scales = tile[128:144].astype(jnp.float32)
    parts = []
    for q in (0, 1):
        w = tile[64 * q:64 * q + 64].astype(jnp.float32)
        size = jnp.exp(jnp.log(jnp.maximum(jnp.abs(w), 1.2e-38)) * (1.0 / POWER))
        parts.append(jnp.where(w < 0.0, -size, size) * (scales[8 * q:8 * q + 1] * (1.0 / LIFT)))
    return jnp.concatenate(parts, axis=1)


def kernel(
    tokens, hid_count, feat_count,
    x_hbm, g_hbm, hs_hbm, fs_hbm,
    upd_ref, hid_ref, feat_ref, rms_ref,
    hs, hx, fs, gv, gt, xp, pb, sb4, rb4, sb, rb, fin, yr, ga, pm, ar, tile, racc, cr, tr,
    lsem, gsend, grecv, crecv, ssem4, rsem4, ssem, rsem, ysend, yrecv, asend, arecv, bsend, brecv,
    hsem, psend, precv, csend, csrecv, tsend, trecv,
):
    r = lax.axis_index("row")
    c = lax.axis_index("col")
    x, yl, k = r // 4, rem(r // 2, 2), rem(r, 2)
    yh, z = c // 8, rem(c, 8)
    part = 2 * z + yh

    def row_of(dx, dy, kk):
        return rem(x + dx, 4) * 4 + rem(yl + dy, 2) * 2 + kk

    def remote(src, dst, send, recv, dev):
        return pltpu.make_async_remote_copy(
            src_ref=src, dst_ref=dst, send_sem=send, recv_sem=recv,
            device_id=dev, device_id_type=MESH,
        )

    copy_x = pltpu.make_async_copy(x_hbm, xp.at[0, k], lsem.at[0])
    copy_x.start()
    copy_g = pltpu.make_async_copy(g_hbm, gv, lsem.at[1])
    copy_g.start()
    copy_hs = pltpu.make_async_copy(hs_hbm, hs, lsem.at[2])
    copy_hs.start()
    copy_fs = pltpu.make_async_copy(fs_hbm, fs, lsem.at[3])
    copy_fs.start()

    barrier = pltpu.get_barrier_semaphore()
    diagonal = r == c
    for i in range(1, 16):
        pl.semaphore_signal(barrier, inc=1, device_id=(rem(r + i, 16), c), device_id_type=MESH)
        pl.semaphore_signal(barrier, inc=1, device_id=(r, rem(c + i, 16)), device_id_type=MESH)

    @pl.when(jnp.logical_not(diagonal))
    def _():
        pl.semaphore_signal(barrier, inc=1, device_id=(c, r), device_id_type=MESH)

    copy_x.wait()
    pl.semaphore_wait(barrier, jnp.where(diagonal, 30, 31))

    east = (row_of(1, 0, k), c)
    west = (row_of(3, 0, k), c)
    side = (row_of(0, 1, k), c)
    mate = (row_of(0, 0, 1 - k), c)
    half = tokens // 2
    whole, low, high = pl.ds(0, tokens), pl.ds(0, half), pl.ds(half, half)

    def send_block(src_slot, dst_slot, rows, send, recv, dev):
        return remote(xp.at[src_slot, k, rows], xp.at[dst_slot, k, rows], gsend.at[send], grecv.at[recv], dev)

    def mate_copy(slot):
        return remote(xp.at[slot, k], xp.at[slot, k], gsend.at[8 + slot], crecv.at[slot], mate)

    sends = {
        "e0": send_block(0, 3, whole, 0, 3, east),
        "w0": send_block(0, 2, whole, 1, 2, west),
        "s0": send_block(0, 1, whole, 2, 1, side),
        "e1": send_block(1, 6, whole, 3, 6, east),
        "w1": send_block(1, 5, whole, 4, 5, west),
        "e3": send_block(3, 4, low, 5, 4, east),
        "w2": send_block(2, 4, high, 6, 0, west),
        "s4": send_block(4, 7, whole, 7, 7, side),
    }

    def wait_block(slot):
        if slot == 4:
            send_block(4, 4, low, 0, 4, east).wait_recv()
            send_block(4, 4, high, 0, 0, east).wait_recv()
        else:
            send_block(slot, slot, whole, 0, slot, east).wait_recv()

    def wait_mate(slot):
        remote(xp.at[slot, 1 - k], xp.at[slot, 1 - k], gsend.at[0], crecv.at[slot], mate).wait_recv()

    for name in ("e0", "w0", "s0"):
        sends[name].start()
    mate_copy(0).start()

    far = 2 * rem(r, 8) + r // 8
    copy_hs.wait()
    hx_copy = remote(hs.at[far // 4], hx, hsem.at[0], hsem.at[1], (c, r))

    @pl.when(diagonal)
    def _():
        hx[...] = hs[part // 4]

    @pl.when(jnp.logical_not(diagonal))
    def _():
        hx_copy.start()

    copy_g.wait()
    copy_fs.wait()
    gt[...] = gv[...].T
    racc[...] = jnp.zeros_like(racc)

    def z_dev(sign):
        return (r, yh * 8 + rem(z + sign + 8, 8))

    def first_copy(s, sign):
        return remote(sb4.at[s], rb4.at[s], ssem4.at[s], rsem4.at[s], z_dev(sign))

    def span_copy(t, way, first, rows):
        at = pl.ds(first, rows)
        return remote(sb.at[t, way, at], rb.at[t, way, at], ssem.at[t, way], rsem.at[t, way], z_dev(1 - 2 * way))

    def spans(t, act):
        for begin, end, first, rows in SPANS:
            @pl.when(jnp.logical_and(t >= begin, t <= end))
            def _():
                for way in (0, 1):
                    act(span_copy(t, way, first, rows))

    def chunk(s, offset):
        rows = pl.ds(pl.multiple_of(rem(z + offset + 8, 8) * 64, 64), 64)
        return pb[s, rows, :]

    def put(t, way, d, value):
        sb[t, way, TILE * (d - 1):TILE * d] = encode(value)

    def got(t, way, d):
        return decode(rb[t, way, TILE * (d - 1):TILE * d])

    def slot_offset(p):
        dy = jnp.where(jnp.logical_or(p == 1, p >= 5), 1, 0)
        one = jnp.logical_or(p == 2, p == 5)
        three = jnp.logical_or(p == 3, p == 6)
        two = jnp.logical_or(p == 4, p == 7)
        dx = jnp.where(one, 1, 0) + jnp.where(two, 2, 0) + jnp.where(three, 3, 0)
        return dx, dy

    y_mate = (r, (1 - yh) * 8 + z)

    def y_copy(s):
        rows = pl.ds(pl.multiple_of((1 - yh) * 32, 32), 32)
        return remote(fin.at[s, rows], yr.at[s], ysend.at[s], yrecv.at[s], y_mate)

    def a_copy(s, kk, f):
        return remote(ga.at[s, kk], ar.at[r, 0:32], asend.at[s, kk], arecv.at[r], (f, c))

    def p_copy(s, kk, f):
        return remote(pm.at[s, kk], ar.at[r, 32:40], psend.at[s, kk], precv.at[r], (f, c))

    def mine(s, kk):
        return jnp.logical_and(s == 0, k == kk)

    def within(s):
        return jnp.logical_and(s >= 0, s < PAIRS)

    def step(t, carry):
        spans(t - 2, lambda copy: copy.wait_recv())
        s0 = t - 8

        @pl.when(within(s0))
        def _():
            fin[s0] = chunk(s0, 0) + got(t - 2, 0, 1) + got(t - 2, 1, 1)
            y_copy(s0).start()

        for d in (1, 2):
            s = t - 8 + 2 * d

            @pl.when(within(s))
            def _():
                for way in (0, 1):
                    put(t, way, d, chunk(s, (1 - 2 * way) * d) + got(t - 2, way, d + 1))

        s3 = t - 2

        @pl.when(within(s3))
        def _():
            first_copy(s3, 1).wait_recv()
            for way in (0, 1):
                long = rem(s3, 2) == way

                @pl.when(long)
                def _():
                    put(t, way, 3, chunk(s3, (1 - 2 * way) * 3) + decode(rb4[s3]))

                @pl.when(jnp.logical_not(long))
                def _():
                    put(t, way, 3, chunk(s3, (1 - 2 * way) * 3))

        spans(t, lambda copy: copy.start())

        @pl.when(t == 1)
        def _():
            wait_block(1)
            mate_copy(1).start()
            wait_block(3)
            sends["e3"].start()
            mate_copy(3).start()
            wait_block(2)
            sends["w2"].start()
            mate_copy(2).start()
            sends["e1"].start()
            sends["w1"].start()

        @pl.when(t == 3)
        def _():
            wait_block(4)
            sends["s4"].start()
            mate_copy(4).start()

        for slot in (5, 6, 7):
            @pl.when(t == slot)
            def _():
                wait_block(slot)
                mate_copy(slot).start()

        @pl.when(t < PAIRS)
        def _():
            wait_mate(t)
            both = jnp.concatenate([xp[t, 0], xp[t, 1]], axis=1)
            pb[t] = jnp.dot(gt[...], both, preferred_element_type=jnp.float32)
            sb4[t] = encode(chunk(t, 4))
            first_copy(t, 1 - 2 * rem(t, 2)).start()

        sy = t - 9

        @pl.when(within(sy))
        def _():
            y_copy(sy).wait_recv()
            rows = pl.ds(pl.multiple_of(yh * 32, 32), 32)
            g = fin[sy, rows, :] + yr[sy]
            racc[...] += g * g + 1e-30
            dx, dy = slot_offset(sy)
            for kk in (0, 1):
                ga[sy, kk] = g[:, kk * 128:(kk + 1) * 128]

                @pl.when(mine(sy, kk))
                def _():
                    ar[r, 0:32] = g[:, kk * 128:(kk + 1) * 128]

                @pl.when(jnp.logical_not(mine(sy, kk)))
                def _():
                    a_copy(sy, kk, row_of(dx, dy, kk)).start()

        return carry

    lax.fori_loop(0, STEPS + 1, step, 0)

    @pl.when(jnp.logical_not(diagonal))
    def _():
        hx_copy.wait_recv()

    sums = jnp.sum(racc[...], axis=1, keepdims=True)
    lane = lax.broadcasted_iota(jnp.int32, (32, 128), 1)
    line = lax.broadcasted_iota(jnp.int32, (32, 128), 0)
    place = lane == line + rem(part, 4) * 32
    old = jnp.sum(jnp.where(place, hx[...], 0.0), axis=1, keepdims=True)
    hid = decay_rate * old + (1.0 - decay_rate) * (sums / feat_count)
    hid_row = jnp.sum(jnp.where(place, hid, 0.0), axis=0, keepdims=True)
    hid_sum = jnp.full((1, 128), jnp.sum(hid), jnp.float32)
    inverse = 1.0 / hid

    def p_step(s, carry):
        dx, dy = slot_offset(s)
        for kk in (0, 1):
            sq = ga[s, kk] * ga[s, kk]
            pm[s, kk, 0:1] = hid_row
            pm[s, kk, 1:2] = jnp.sum(sq + 1e-30, axis=0, keepdims=True)
            pm[s, kk, 2:3] = jnp.sum(sq * inverse, axis=0, keepdims=True)
            pm[s, kk, 3:4] = hid_sum
            pm[s, kk, 4:8] = jnp.zeros((4, 128), jnp.float32)

            @pl.when(mine(s, kk))
            def _():
                ar[r, 32:40] = pm[s, kk]

            @pl.when(jnp.logical_not(mine(s, kk)))
            def _():
                p_copy(s, kk, row_of(dx, dy, kk)).start()

        return carry

    lax.fori_loop(0, PAIRS, p_step, 0)

    def wait_p(i, carry):
        q = rem(r + i, 16)
        remote(ar.at[q, 32:40], ar.at[q, 32:40], psend.at[0, 0], precv.at[q], mate).wait_recv()
        return carry

    lax.fori_loop(1, 16, wait_p, 0)
    cr[c] = jnp.sum(ar[:, 32:40], axis=0)

    def c_copy(i):
        return remote(cr.at[c], cr.at[c], csend.at[i], csrecv.at[c], (r, rem(c + i, 16)))

    for i in (8, 7, 9, 4, 12, 5, 11, 3, 13, 6, 10, 2, 14, 1, 15):
        c_copy(i).start()

    def b_copy(q):
        return remote(ar.at[q], tile.at[part], bsend.at[q], brecv.at[part], (r, q))

    def wait_a(q):
        remote(ar.at[q, 0:32], ar.at[q, 0:32], asend.at[0, 0], arecv.at[q], mate).wait_recv()

    def b_step(i, carry):
        q = rem(c + i, 16)

        @pl.when(q != r)
        def _():
            wait_a(q)

        @pl.when(i == 0)
        def _():
            tile[part] = ar[c]

        @pl.when(i > 0)
        def _():
            b_copy(q).start()

        return carry

    lax.fori_loop(0, 16, b_step, 0)

    def wait_c(i, carry):
        q = rem(c + i, 16)
        remote(cr.at[q], cr.at[q], csend.at[0], csrecv.at[q], mate).wait_recv()
        return carry

    lax.fori_loop(1, 16, wait_c, 0)
    both = jnp.sum(cr[...], axis=0)
    feat = decay_rate * fs[...] + (1.0 - decay_rate) * (both[1:2, :] / hid_count)
    feat_ref[...] = feat
    hid_mean = both[3:4, :] / hid_count
    tr[r] = jnp.full((1, 128), jnp.sum(both[2:3, :] / feat), jnp.float32)

    def t_copy(i):
        return remote(tr.at[r], tr.at[r], tsend.at[i], trecv.at[r], (rem(r + i, 16), c))

    for i in range(1, 16):
        t_copy(i).start()

    def drain(s, carry):
        first_copy(s, 1).wait_send()
        y_copy(s).wait_send()
        for kk in (0, 1):
            @pl.when(jnp.logical_not(mine(s, kk)))
            def _():
                a_copy(s, kk, r).wait_send()
                p_copy(s, kk, r).wait_send()
        mate_copy(s).wait_send()
        return carry

    lax.fori_loop(0, PAIRS, drain, 0)

    def drain_spans(t, carry):
        spans(t, lambda copy: copy.wait_send())
        return carry

    lax.fori_loop(2, STEPS - 2, drain_spans, 0)
    for one in sends.values():
        one.wait_send()

    @pl.when(jnp.logical_not(diagonal))
    def _():
        hx_copy.wait_send()

    def finish_b(i, carry):
        b_copy(rem(c + i, 16)).wait_send()
        c_copy(i).wait_send()
        q = rem(part + i, 16)
        remote(tile.at[q], tile.at[q], bsend.at[0], brecv.at[q], mate).wait_recv()
        return carry

    lax.fori_loop(1, 16, finish_b, 0)
    eye = lax.broadcasted_iota(jnp.int32, (128, 128), 0) == lax.broadcasted_iota(jnp.int32, (128, 128), 1)
    columns = []
    for q in range(4):
        line_q = tile[4 * q, 32:33] + tile[4 * q + 1, 32:33] + tile[4 * q + 2, 32:33] + tile[4 * q + 3, 32:33]
        hid_ref[q:q + 1, :] = line_q
        columns.append(lax.rsqrt(jnp.sum(jnp.where(eye, line_q, 0.0), axis=1, keepdims=True)))

    def wait_t(i, carry):
        q = rem(r + i, 16)
        remote(tr.at[q], tr.at[q], tsend.at[0], trecv.at[q], mate).wait_recv()
        t_copy(i).wait_send()
        return carry

    lax.fori_loop(1, 16, wait_t, 0)
    mean = hid_mean * jnp.sum(tr[...], axis=0) / (hid_count * feat_count)
    rms = jnp.sqrt(mean)
    rms_ref[...] = rms
    across = jnp.sqrt(hid_mean / feat) / jnp.maximum(1.0, rms)
    for q in range(4):
        g = tile[4 * q:4 * q + 4, 0:32].reshape(128, 128)
        upd_ref[128 * q:128 * q + 128, :] = g * columns[q] * across


def writer(a, b, c, d, oa, ob, oc, od, sem):
    copies = [pltpu.make_async_copy(src, dst, sem.at[i]) for i, (src, dst) in enumerate(((a, oa), (b, ob), (c, oc), (d, od)))]
    for copy in copies:
        copy.start()
    for copy in copies:
        copy.wait()


def body(layer_input, grad_output, hid_state, feat_state):
    tokens = layer_input.shape[0]
    hid_count, feat_count = 8192.0, 2048.0
    vm = pl.BlockSpec(memory_space=pltpu.VMEM)
    hbm = pl.BlockSpec(memory_space=pl.ANY)
    f32, bf16 = jnp.float32, jnp.bfloat16
    dma = pltpu.SemaphoreType.DMA
    shapes = (
        jax.ShapeDtypeStruct((512, 128), f32),
        jax.ShapeDtypeStruct((4, 128), f32),
        jax.ShapeDtypeStruct((1, 128), f32),
        jax.ShapeDtypeStruct((1, 128), f32),
    )
    outs = pl.pallas_call(
        functools.partial(kernel, tokens, hid_count, feat_count),
        name="optimizer_step",
        out_shape=shapes,
        in_specs=[hbm, hbm, hbm, hbm],
        out_specs=(vm, vm, vm, vm),
        scratch_shapes=[
            pltpu.VMEM((4, 1, 128), f32),
            pltpu.VMEM((1, 128), f32),
            pltpu.VMEM((1, 128), f32),
            pltpu.VMEM((tokens, 512), bf16),
            pltpu.VMEM((512, tokens), bf16),
            pltpu.VMEM((PAIRS, 2, tokens, 128), bf16),
            pltpu.VMEM((PAIRS, 512, 256), f32),
            pltpu.VMEM((PAIRS, TILE, 128), MSG),
            pltpu.VMEM((PAIRS, TILE, 128), MSG),
            pltpu.VMEM((STEPS, 2, 3 * TILE, 128), MSG),
            pltpu.VMEM((STEPS, 2, 3 * TILE, 128), MSG),
            pltpu.VMEM((PAIRS, 64, 256), f32),
            pltpu.VMEM((PAIRS, 32, 256), f32),
            pltpu.VMEM((PAIRS, 2, 32, 128), f32),
            pltpu.VMEM((PAIRS, 2, 8, 128), f32),
            pltpu.VMEM((16, 40, 128), f32),
            pltpu.VMEM((16, 40, 128), f32),
            pltpu.VMEM((32, 256), f32),
            pltpu.VMEM((16, 8, 128), f32),
            pltpu.VMEM((16, 1, 128), f32),
            dma((4,)), dma((16,)), dma((8,)), dma((PAIRS,)),
            dma((PAIRS,)), dma((PAIRS,)), dma((STEPS, 2)), dma((STEPS, 2)), dma((PAIRS,)), dma((PAIRS,)),
            dma((PAIRS, 2)), dma((16,)), dma((16,)), dma((16,)),
            dma((2,)), dma((PAIRS, 2)), dma((16,)), dma((16,)), dma((16,)), dma((16,)), dma((16,)),
        ],
        compiler_params=pltpu.CompilerParams(
            collective_id=0, has_side_effects=True, vmem_limit_bytes=62 << 20
        ),
    )(layer_input, grad_output, hid_state.reshape(4, 1, 128), feat_state.reshape(1, 128))
    update, hid, feat, rms = pl.pallas_call(
        writer,
        name="write_results",
        out_shape=shapes,
        in_specs=[vm] * 4,
        out_specs=[hbm] * 4,
        scratch_shapes=[dma((4,))],
        compiler_params=pltpu.CompilerParams(vmem_limit_bytes=62 << 20),
    )(*outs)
    return update, hid.reshape(512), feat.reshape(128), rms[0, 0]


def solution(mesh):
    in_specs = (P("col", "row"), P("col", "row"), P("col"), P("row"))
    out_specs = (P("col", "row"), P("col"), P("row"), P())
    return jax.shard_map(body, mesh=mesh, in_specs=in_specs, out_specs=out_specs, check_vma=False)
```

time: 108 us -> 87.5 us (0.81)
  Pallas kernels: 100 us -> 86.7 us
  local copies, waits for them, and re-layouts: 5.53 us -> 0 us
  between operations: 1.82 us -> 0.64 us
    pallas_call x1, Pallas kernels: 100 us -> 85 us  [body(): pl.pallas_call(functools.partial(kernel, tokens, hid_count, feat_count),...]
    unnamed x11 -> x0, local copies, waits for them, and re-layouts: 5.53 us -> none
    pallas_call x0 -> x1, Pallas kernels: none -> 1.7 us  [body(): pl.pallas_call(writer, name='write_results', out_shape=shapes, in_specs=[...]
where the time goes in v2:
time: 87.5 us; the launch traced here: 87.4 us
  Pallas kernels  86.7 us (99%)
    pallas_call x1, Pallas kernels, body(): pl.pallas_call(functools.partial(kernel, tokens, hid_count, feat_count),...  85 us

profile of v2, /device:TPU:1, one launch (start us, length us, event | category | flops | bytes accessed | tf_op | source)
XLA Modules:
  0.0 87.4 jit_solution(1443075691591543053)
XLA Ops:
  0.6 85.0 %optimizer_step.1 = (f32[512,128]{1,0:T(8,128)}, f32[4,128]{1,0:T(4,128)}, f32[1,128]{1,0:T(1,128)}, f32[1,128]{1,0:T(1,128)}) custom-call(bf16[1536,128]{1,0:T(8,128)(2,1)} %x_hbm.1, bf16[1536,512]{1,0:T(8,128)(2,1)} %g_hbm.1, f32[4,1,128]{2,1,0:T(1,128)} %bitcast.6, f32[1,128]{1,0:T(1,128)} %bitcast.7), custom_call_target="tpu_custom_call" | custom-call | tf_op jit(solution)/shard_map/optimizer_step/pallas_call | solution.py:460
  85.7 1.7 %write_results.1 = (f32[512,128]{1,0:T(8,128)}, f32[4,128]{1,0:T(4,128)}, f32[1,128]{1,0:T(1,128)}, f32[1,128]{1,0:T(1,128)}) custom-call(f32[512,128]{1,0:T(8,128)} %get-tuple-element.12.a, f32[4,128]{1,0:T(4,128)} %get-tuple-element.13.b, f32[1,128]{1,0:T(1,128)} %get-tuple-element.14.c, f32[1,128]{1,0:T(1,128)} %get-tuple-element.15.d), custom_call_target="tpu_custom_call" | custom-call | tf_op jit(solution)/shard_map/write_results/pallas_call | solution.py:496

commit v3 on v2

--- a/solution.py
+++ b/solution.py
@@ -9,12 +9,19 @@
 decay_rate = 0.8415106807538887
 MESH = pl.DeviceIdType.MESH
 PAIRS = 8
-STEPS = 2 * PAIRS
 MSG = jnp.bfloat16
 POWER = 13
 LIFT = 2.0 ** 9
 TILE = 144
-SPANS = ((2, 3, 2 * TILE, TILE), (4, 5, TILE, 2 * TILE), (6, 9, 0, 3 * TILE), (10, 11, 0, 2 * TILE), (12, 13, 0, TILE))
+PLAN = (
+    (0, 0), (1, 0), (2, 0), (6, 0), (0, 1), (3, 0), (0, 2), (0, 3),
+    (1, 1), (4, 0), (1, 2), (1, 3), (7, 0), (2, 1), (5, 0), (9, 0), (0, 4),
+    (2, 2), (2, 3), (3, 1), (1, 4), (3, 2), (8, 5), (8, 6), (3, 3),
+    (4, 1), (0, 5), (0, 6), (2, 4), (4, 2), (8, 7), (4, 3), (5, 1),
+    (0, 7), (1, 5), (1, 6), (3, 4), (5, 2), (5, 3), (1, 7), (2, 5),
+    (2, 6), (4, 4), (2, 7), (3, 5), (3, 6), (5, 4), (3, 7), (4, 5),
+    (4, 6), (4, 7), (5, 5), (5, 6), (5, 7),
+)
 
 
 def rem(a, n):
@@ -46,9 +53,9 @@
     tokens, hid_count, feat_count,
     x_hbm, g_hbm, hs_hbm, fs_hbm,
     upd_ref, hid_ref, feat_ref, rms_ref,
-    hs, hx, fs, gv, gt, xp, pb, sb4, rb4, sb, rb, fin, yr, ga, pm, ar, tile, racc, cr, tr,
-    lsem, gsend, grecv, crecv, ssem4, rsem4, ssem, rsem, ysend, yrecv, asend, arecv, bsend, brecv,
-    hsem, psend, precv, csend, csrecv, tsend, trecv,
+    hs, hx, fs, gv, gt, xp, pb, sb, rb, fin, yr, ga, pm, ar, tile, racc, cr, tr,
+    lsem, gsend, grecv, crecv, ssem, rsem, ysend, yrecv, asend, arecv, bsend, brecv,
+    hsend, hrecv, psend, precv, csend, csrecv, tsend, trecv,
 ):
     r = lax.axis_index("row")
     c = lax.axis_index("col")
@@ -76,21 +83,19 @@
 
     barrier = pltpu.get_barrier_semaphore()
     diagonal = r == c
-    for i in range(1, 16):
-        pl.semaphore_signal(barrier, inc=1, device_id=(rem(r + i, 16), c), device_id_type=MESH)
-        pl.semaphore_signal(barrier, inc=1, device_id=(r, rem(c + i, 16)), device_id_type=MESH)
-
-    @pl.when(jnp.logical_not(diagonal))
-    def _():
-        pl.semaphore_signal(barrier, inc=1, device_id=(c, r), device_id_type=MESH)
-
-    copy_x.wait()
-    pl.semaphore_wait(barrier, jnp.where(diagonal, 30, 31))
-
     east = (row_of(1, 0, k), c)
     west = (row_of(3, 0, k), c)
     side = (row_of(0, 1, k), c)
     mate = (row_of(0, 0, 1 - k), c)
+    y_mate = (r, (1 - yh) * 8 + z)
+    up = (r, yh * 8 + rem(z + 1, 8))
+    down = (r, yh * 8 + rem(z + 7, 8))
+    peers = (east, west, side, mate, y_mate, up, down)
+    for dev in peers:
+        pl.semaphore_signal(barrier, inc=1, device_id=dev, device_id_type=MESH)
+    copy_x.wait()
+    pl.semaphore_wait(barrier, len(peers))
+
     half = tokens // 2
     whole, low, high = pl.ds(0, tokens), pl.ds(0, half), pl.ds(half, half)
 
@@ -125,49 +130,42 @@
         sends[name].start()
     mate_copy(0).start()
 
-    far = 2 * rem(r, 8) + r // 8
-    copy_hs.wait()
-    hx_copy = remote(hs.at[far // 4], hx, hsem.at[0], hsem.at[1], (c, r))
-
-    @pl.when(diagonal)
-    def _():
-        hx[...] = hs[part // 4]
-
-    @pl.when(jnp.logical_not(diagonal))
-    def _():
-        hx_copy.start()
+    def hx_copy(i):
+        to = rem(c + i, 16)
+        return remote(hs.at[(2 * rem(to, 8) + to // 8) // 4], hx, hsend.at[i], hrecv, (r, to))
 
     copy_g.wait()
     copy_fs.wait()
+    copy_hs.wait()
     gt[...] = gv[...].T
     racc[...] = jnp.zeros_like(racc)
 
     def z_dev(sign):
         return (r, yh * 8 + rem(z + sign + 8, 8))
 
-    def first_copy(s, sign):
-        return remote(sb4.at[s], rb4.at[s], ssem4.at[s], rsem4.at[s], z_dev(sign))
-
-    def span_copy(t, way, first, rows):
-        at = pl.ds(first, rows)
-        return remote(sb.at[t, way, at], rb.at[t, way, at], ssem.at[t, way], rsem.at[t, way], z_dev(1 - 2 * way))
-
-    def spans(t, act):
-        for begin, end, first, rows in SPANS:
-            @pl.when(jnp.logical_and(t >= begin, t <= end))
-            def _():
-                for way in (0, 1):
-                    act(span_copy(t, way, first, rows))
+    def message(s, m, sign):
+        return remote(sb.at[s, m], rb.at[s, m], ssem.at[s, m], rsem.at[s, m], z_dev(sign))
 
     def chunk(s, offset):
         rows = pl.ds(pl.multiple_of(rem(z + offset + 8, 8) * 64, 64), 64)
         return pb[s, rows, :]
 
-    def put(t, way, d, value):
-        sb[t, way, TILE * (d - 1):TILE * d] = encode(value)
-
-    def got(t, way, d):
-        return decode(rb[t, way, TILE * (d - 1):TILE * d])
+    def put(s, m, sign, value):
+        sb[s, m] = encode(value)
+        message(s, m, sign).start()
+
+    def got(s, m):
+        message(s, m, 1).wait_recv()
+        return decode(rb[s, m])
+
+    words = [sum((8 * kind + s) << (8 * i) for i, (kind, s) in enumerate(PLAN[at:at + 4])) for at in range(0, len(PLAN), 4)]
+
+    def planned(t):
+        word = jnp.int32(0)
+        for i, value in enumerate(words):
+            word = jnp.where(t // 4 == i, value, word)
+        code = rem(lax.shift_right_logical(word, 8 * rem(t, 4)), 256)
+        return code // 8, rem(code, 8)
 
     def slot_offset(p):
         dy = jnp.where(jnp.logical_or(p == 1, p >= 5), 1, 0)
@@ -177,8 +175,6 @@
         dx = jnp.where(one, 1, 0) + jnp.where(two, 2, 0) + jnp.where(three, 3, 0)
         return dx, dy
 
-    y_mate = (r, (1 - yh) * 8 + z)
-
     def y_copy(s):
         rows = pl.ds(pl.multiple_of((1 - yh) * 32, 32), 32)
         return remote(fin.at[s, rows], yr.at[s], ysend.at[s], yrecv.at[s], y_mate)
@@ -192,45 +188,59 @@
     def mine(s, kk):
         return jnp.logical_and(s == 0, k == kk)
 
-    def within(s):
-        return jnp.logical_and(s >= 0, s < PAIRS)
-
     def step(t, carry):
-        spans(t - 2, lambda copy: copy.wait_recv())
-        s0 = t - 8
-
-        @pl.when(within(s0))
-        def _():
-            fin[s0] = chunk(s0, 0) + got(t - 2, 0, 1) + got(t - 2, 1, 1)
-            y_copy(s0).start()
-
-        for d in (1, 2):
-            s = t - 8 + 2 * d
-
-            @pl.when(within(s))
-            def _():
-                for way in (0, 1):
-                    put(t, way, d, chunk(s, (1 - 2 * way) * d) + got(t - 2, way, d + 1))
-
-        s3 = t - 2
-
-        @pl.when(within(s3))
-        def _():
-            first_copy(s3, 1).wait_recv()
-            for way in (0, 1):
-                long = rem(s3, 2) == way
+        kind, s = planned(t)
+
+        @pl.when(kind == 0)
+        def _():
+            wait_mate(s)
+            both = jnp.concatenate([xp[s, 0], xp[s, 1]], axis=1)
+            pb[s] = jnp.dot(gt[...], both, preferred_element_type=jnp.float32)
+            put(s, 0, 1 - 2 * rem(s, 2), chunk(s, 4))
+
+        @pl.when(kind == 1)
+        def _():
+            for way, sign in ((0, 1), (1, -1)):
+                long = rem(s, 2) == way
 
                 @pl.when(long)
                 def _():
-                    put(t, way, 3, chunk(s3, (1 - 2 * way) * 3) + decode(rb4[s3]))
+                    put(s, 1 + way, sign, chunk(s, sign * 3) + got(s, 0))
 
                 @pl.when(jnp.logical_not(long))
                 def _():
-                    put(t, way, 3, chunk(s3, (1 - 2 * way) * 3))
-
-        spans(t, lambda copy: copy.start())
-
-        @pl.when(t == 1)
+                    put(s, 1 + way, sign, chunk(s, sign * 3))
+
+        @pl.when(jnp.logical_or(kind == 2, kind == 3))
+        def _():
+            d = 4 - kind
+            for way, sign in ((0, 1), (1, -1)):
+                put(s, 7 - 2 * d + way, sign, chunk(s, sign * d) + got(s, 5 - 2 * d + way))
+
+        @pl.when(kind == 4)
+        def _():
+            fin[s] = chunk(s, 0) + got(s, 5) + got(s, 6)
+            y_copy(s).start()
+
+        @pl.when(kind == 5)
+        def _():
+            y_copy(s).wait_recv()
+            rows = pl.ds(pl.multiple_of(yh * 32, 32), 32)
+            g = fin[s, rows, :] + yr[s]
+            racc[...] += g * g + 1e-30
+            dx, dy = slot_offset(s)
+            for kk in (0, 1):
+                ga[s, kk] = g[:, kk * 128:(kk + 1) * 128]
+
+                @pl.when(mine(s, kk))
+                def _():
+                    ar[r, 0:32] = g[:, kk * 128:(kk + 1) * 128]
+
+                @pl.when(jnp.logical_not(mine(s, kk)))
+                def _():
+                    a_copy(s, kk, row_of(dx, dy, kk)).start()
+
+        @pl.when(kind == 6)
         def _():
             wait_block(1)
             mate_copy(1).start()
@@ -243,53 +253,30 @@
             sends["e1"].start()
             sends["w1"].start()
 
-        @pl.when(t == 3)
+        @pl.when(kind == 7)
         def _():
             wait_block(4)
             sends["s4"].start()
             mate_copy(4).start()
 
-        for slot in (5, 6, 7):
-            @pl.when(t == slot)
-            def _():
-                wait_block(slot)
-                mate_copy(slot).start()
-
-        @pl.when(t < PAIRS)
-        def _():
-            wait_mate(t)
-            both = jnp.concatenate([xp[t, 0], xp[t, 1]], axis=1)
-            pb[t] = jnp.dot(gt[...], both, preferred_element_type=jnp.float32)
-            sb4[t] = encode(chunk(t, 4))
-            first_copy(t, 1 - 2 * rem(t, 2)).start()
-
-        sy = t - 9
-
-        @pl.when(within(sy))
-        def _():
-            y_copy(sy).wait_recv()
-            rows = pl.ds(pl.multiple_of(yh * 32, 32), 32)
-            g = fin[sy, rows, :] + yr[sy]
-            racc[...] += g * g + 1e-30
-            dx, dy = slot_offset(sy)
-            for kk in (0, 1):
-                ga[sy, kk] = g[:, kk * 128:(kk + 1) * 128]
-
-                @pl.when(mine(sy, kk))
-                def _():
-                    ar[r, 0:32] = g[:, kk * 128:(kk + 1) * 128]
-
-                @pl.when(jnp.logical_not(mine(sy, kk)))
-                def _():
-                    a_copy(sy, kk, row_of(dx, dy, kk)).start()
-
-        return carry
-
-    lax.fori_loop(0, STEPS + 1, step, 0)
+        @pl.when(jnp.logical_and(kind == 9, diagonal))
+        def _():
+            hx[...] = hs[part // 4]
+            for i in range(1, 16):
+                hx_copy(i).start()
+
+        @pl.when(kind == 8)
+        def _():
+            send_block(s, s, whole, 0, s, east).wait_recv()
+            mate_copy(s).start()
+
+        return carry
+
+    lax.fori_loop(0, len(PLAN), step, 0)
 
     @pl.when(jnp.logical_not(diagonal))
     def _():
-        hx_copy.wait_recv()
+        hx_copy(1).wait_recv()
 
     sums = jnp.sum(racc[...], axis=1, keepdims=True)
     lane = lax.broadcasted_iota(jnp.int32, (32, 128), 1)
@@ -323,6 +310,22 @@
 
     lax.fori_loop(0, PAIRS, p_step, 0)
 
+    def drain(s, carry):
+        for m in range(7):
+            message(s, m, 1).wait_send()
+        y_copy(s).wait_send()
+        mate_copy(s).wait_send()
+        for kk in (0, 1):
+            @pl.when(jnp.logical_not(mine(s, kk)))
+            def _():
+                a_copy(s, kk, r).wait_send()
+
+        return carry
+
+    lax.fori_loop(0, PAIRS, drain, 0)
+    for one in sends.values():
+        one.wait_send()
+
     def wait_p(i, carry):
         q = rem(r + i, 16)
         remote(ar.at[q, 32:40], ar.at[q, 32:40], psend.at[0, 0], precv.at[q], mate).wait_recv()
@@ -380,30 +383,20 @@
     for i in range(1, 16):
         t_copy(i).start()
 
-    def drain(s, carry):
-        first_copy(s, 1).wait_send()
-        y_copy(s).wait_send()
+    def drain_p(s, carry):
         for kk in (0, 1):
             @pl.when(jnp.logical_not(mine(s, kk)))
             def _():
-                a_copy(s, kk, r).wait_send()
                 p_copy(s, kk, r).wait_send()
-        mate_copy(s).wait_send()
-        return carry
-
-    lax.fori_loop(0, PAIRS, drain, 0)
-
-    def drain_spans(t, carry):
-        spans(t, lambda copy: copy.wait_send())
-        return carry
-
-    lax.fori_loop(2, STEPS - 2, drain_spans, 0)
-    for one in sends.values():
-        one.wait_send()
-
-    @pl.when(jnp.logical_not(diagonal))
+
+        return carry
+
+    lax.fori_loop(0, PAIRS, drain_p, 0)
+
+    @pl.when(diagonal)
     def _():
-        hx_copy.wait_send()
+        for i in range(1, 16):
+            hx_copy(i).wait_send()
 
     def finish_b(i, carry):
         b_copy(rem(c + i, 16)).wait_send()
@@ -423,10 +416,11 @@
     def wait_t(i, carry):
         q = rem(r + i, 16)
         remote(tr.at[q], tr.at[q], tsend.at[0], trecv.at[q], mate).wait_recv()
+        return carry
+
+    lax.fori_loop(1, 16, wait_t, 0)
+    for i in range(1, 16):
         t_copy(i).wait_send()
-        return carry
-
-    lax.fori_loop(1, 16, wait_t, 0)
     mean = hid_mean * jnp.sum(tr[...], axis=0) / (hid_count * feat_count)
     rms = jnp.sqrt(mean)
     rms_ref[...] = rms
@@ -471,10 +465,8 @@
             pltpu.VMEM((512, tokens), bf16),
             pltpu.VMEM((PAIRS, 2, tokens, 128), bf16),
             pltpu.VMEM((PAIRS, 512, 256), f32),
-            pltpu.VMEM((PAIRS, TILE, 128), MSG),
-            pltpu.VMEM((PAIRS, TILE, 128), MSG),
-            pltpu.VMEM((STEPS, 2, 3 * TILE, 128), MSG),
-            pltpu.VMEM((STEPS, 2, 3 * TILE, 128), MSG),
+            pltpu.VMEM((PAIRS, 7, TILE, 128), MSG),
+            pltpu.VMEM((PAIRS, 7, TILE, 128), MSG),
             pltpu.VMEM((PAIRS, 64, 256), f32),
             pltpu.VMEM((PAIRS, 32, 256), f32),
             pltpu.VMEM((PAIRS, 2, 32, 128), f32),
@@ -485,9 +477,9 @@
             pltpu.VMEM((16, 8, 128), f32),
             pltpu.VMEM((16, 1, 128), f32),
             dma((4,)), dma((16,)), dma((8,)), dma((PAIRS,)),
-            dma((PAIRS,)), dma((PAIRS,)), dma((STEPS, 2)), dma((STEPS, 2)), dma((PAIRS,)), dma((PAIRS,)),
+            dma((PAIRS, 7)), dma((PAIRS, 7)), dma((PAIRS,)), dma((PAIRS,)),
             dma((PAIRS, 2)), dma((16,)), dma((16,)), dma((16,)),
-            dma((2,)), dma((PAIRS, 2)), dma((16,)), dma((16,)), dma((16,)), dma((16,)), dma((16,)),
+            dma((16,)), dma, dma((PAIRS, 2)), dma((16,)), dma((16,)), dma((16,)), dma((16,)), dma((16,)),
         ],
         compiler_params=pltpu.CompilerParams(
             collective_id=0, has_side_effects=True, vmem_limit_bytes=62 << 20

time: 87.5 us -> 78.7 us (0.90)
  Pallas kernels: 86.7 us -> 77.9 us
    pallas_call x1, Pallas kernels: 85 us -> 76.2 us  [body(): pl.pallas_call(functools.partial(kernel, tokens, hid_count, feat_count),...]
where the time goes in v3:
time: 78.7 us; the launch traced here: 78.6 us
  Pallas kernels  77.9 us (99%)
    pallas_call x1, Pallas kernels, body(): pl.pallas_call(functools.partial(kernel, tokens, hid_count, feat_count),...  76.2 us
    pallas_call x1, Pallas kernels, body(): pl.pallas_call(writer, name='write_results', out_shape=shapes, in_specs=[...  1.7 us

profile of v3, /device:TPU:1, one launch (start us, length us, event | category | flops | bytes accessed | tf_op | source)
XLA Modules:
  0.0 78.6 jit_solution(13725320891735556873)
XLA Ops:
  0.6 76.2 %optimizer_step.1 = (f32[512,128]{1,0:T(8,128)}, f32[4,128]{1,0:T(4,128)}, f32[1,128]{1,0:T(1,128)}, f32[1,128]{1,0:T(1,128)}) custom-call(bf16[1536,128]{1,0:T(8,128)(2,1)} %x_hbm.1, bf16[1536,512]{1,0:T(8,128)(2,1)} %g_hbm.1, f32[4,1,128]{2,1,0:T(1,128)} %bitcast.6, f32[1,128]{1,0:T(1,128)} %bitcast.7), custom_call_target="tpu_custom_call" | custom-call | tf_op jit(solution)/shard_map/optimizer_step/pallas_call | solution.py:454
  76.9 1.7 %write_results.1 = (f32[512,128]{1,0:T(8,128)}, f32[4,128]{1,0:T(4,128)}, f32[1,128]{1,0:T(1,128)}, f32[1,128]{1,0:T(1,128)}) custom-call(f32[512,128]{1,0:T(8,128)} %get-tuple-element.12.a, f32[4,128]{1,0:T(4,128)} %get-tuple-element.13.b, f32[1,128]{1,0:T(1,128)} %get-tuple-element.14.c, f32[1,128]{1,0:T(1,128)} %get-tuple-element.15.d), custom_call_target="tpu_custom_call" | custom-call | tf_op jit(solution)/shard_map/write_results/pallas_call | solution.py:488

commit v4 on v3

v4 whole, which is shorter than its diff:
```python
import functools
import jax
import jax.numpy as jnp
from jax import lax
from jax.sharding import PartitionSpec as P
from jax.experimental import pallas as pl
from jax.experimental.pallas import tpu as pltpu

decay_rate = 0.8415106807538887
MESH = pl.DeviceIdType.MESH
PAIRS = 8
MSG = jnp.bfloat16
POWER = 13
LIFT = 2.0 ** 9
TILE = 144
HALF = 80
PLAN = (
    (0, 0), (1, 0), (6, 0), (2, 0), (7, 0), (0, 1), (0, 2), (0, 3),
    (10, 0), (8, 5), (3, 0), (1, 1), (0, 5), (1, 2), (8, 6), (8, 4),
    (1, 3), (2, 1), (0, 6), (0, 4), (2, 2), (8, 7), (2, 3), (1, 5),
    (0, 7), (1, 6), (1, 4), (3, 1), (2, 5), (1, 7), (2, 6), (2, 4),
    (3, 2), (3, 3), (2, 7), (3, 5), (3, 6), (3, 4), (4, 0), (9, 0),
    (4, 1), (3, 7), (4, 2), (4, 3), (4, 5), (4, 6), (4, 4), (4, 7),
)


def rem(a, n):
    return lax.rem(a, n)


def encode(value):
    top = jnp.maximum(jnp.max(jnp.abs(value), axis=0, keepdims=True), 1e-30)
    scale = top.astype(MSG).astype(jnp.float32)
    m = value * (LIFT / scale)
    m2 = m * m
    m4 = m2 * m2
    coded = ((m * m4) * (m4 * m4)).astype(MSG)
    scales = [jnp.broadcast_to(scale[:, 128 * q:128 * q + 128], (8, 128)) for q in (0, 1)]
    return jnp.concatenate([coded[:, 0:128], coded[:, 128:256], jnp.concatenate(scales, axis=0).astype(MSG)], axis=0)


def decode(tile):
    n = (tile.shape[0] - 16) // 2
    scales = tile[2 * n:2 * n + 16].astype(jnp.float32)
    parts = []
    for q in (0, 1):
        w = tile[n * q:n * q + n].astype(jnp.float32)
        size = jnp.exp(jnp.log(jnp.maximum(jnp.abs(w), 1.2e-38)) * (1.0 / POWER))
        parts.append(jnp.where(w < 0.0, -size, size) * (scales[8 * q:8 * q + 1] * (1.0 / LIFT)))
    return jnp.concatenate(parts, axis=1)


def kernel(
    tokens, hid_count, feat_count,
    x_hbm, g_hbm, hs_hbm, fs_hbm,
    upd_ref, hid_ref, feat_ref, rms_ref,
    hs, hx, fs, gv, gt, xp, pb, sb, rb, hsb, hrb, ga, fsum, pm, ar, tile, racc, cr, tr,
    lsem, gsend, grecv, msend, crecv, ssem, rsem, hssem, hrsem, asend, arecv, bsend, brecv,
    hsend, hrecv, psend, precv, csend, csrecv, tsend, trecv,
):
    r = lax.axis_index("row")
    c = lax.axis_index("col")
    x, yl, k = r // 4, rem(r // 2, 2), rem(r, 2)
    yh, z = c // 8, rem(c, 8)
    part = 2 * z + yh

    def row_of(dx, dy, kk):
        return rem(x + dx, 4) * 4 + rem(yl + dy, 2) * 2 + kk

    def remote(src, dst, send, recv, dev):
        return pltpu.make_async_remote_copy(
            src_ref=src, dst_ref=dst, send_sem=send, recv_sem=recv,
            device_id=dev, device_id_type=MESH,
        )

    copy_x = pltpu.make_async_copy(x_hbm, xp.at[0, k], lsem.at[0])
    copy_x.start()
    copy_g = pltpu.make_async_copy(g_hbm, gv, lsem.at[1])
    copy_g.start()
    copy_hs = pltpu.make_async_copy(hs_hbm, hs, lsem.at[2])
    copy_hs.start()
    copy_fs = pltpu.make_async_copy(fs_hbm, fs, lsem.at[3])
    copy_fs.start()

    barrier = pltpu.get_barrier_semaphore()
    diagonal = r == c
    east = (row_of(1, 0, k), c)
    west = (row_of(3, 0, k), c)
    side = (row_of(0, 1, k), c)
    mate = (row_of(0, 0, 1 - k), c)
    y_mate = (r, (1 - yh) * 8 + z)
    up = (r, yh * 8 + rem(z + 1, 8))
    down = (r, yh * 8 + rem(z + 7, 8))
    cross_up = (r, (1 - yh) * 8 + rem(z + 1, 8))
    cross_down = (r, (1 - yh) * 8 + rem(z + 7, 8))
    peers = (east, west, side, mate, y_mate, up, down, cross_up, cross_down)
    for dev in peers:
        pl.semaphore_signal(barrier, inc=1, device_id=dev, device_id_type=MESH)
    copy_x.wait()
    pl.semaphore_wait(barrier, len(peers))

    size = tokens // 4
    spans = {
        "a": pl.ds(0, tokens), "l": pl.ds(0, 2 * size), "h": pl.ds(2 * size, 2 * size),
        "l1": pl.ds(0, size), "l2": pl.ds(size, size), "h1": pl.ds(2 * size, size), "h2": pl.ds(3 * size, size),
    }
    routes = {
        "e0h": (0, 3, "h", east), "e0l": (0, 3, "l", east), "w0l": (0, 2, "l", west), "w0h": (0, 2, "h", west),
        "s0l1": (0, 1, "l1", side), "s0h1": (0, 1, "h1", side), "s0l2": (0, 1, "l2", side), "s0h2": (0, 1, "h2", side),
        "e1l1": (1, 6, "l1", east), "e1l2": (1, 6, "l2", east), "w1h1": (1, 5, "h1", west), "w1h2": (1, 5, "h2", west),
        "e3l": (3, 4, "l", east), "w2h": (2, 4, "h", west), "s2l": (2, 5, "l", side), "s3h": (3, 6, "h", side),
        "e6l": (6, 7, "l", east), "w5h": (5, 7, "h", west),
    }
    number = {name: i for i, name in enumerate(routes)}
    arrives = {(there, rows): number[name] for name, (_, there, rows, _) in routes.items()}

    def block_copy(name):
        here, there, rows, dev = routes[name]
        i = number[name]
        return remote(xp.at[here, k, spans[rows]], xp.at[there, k, spans[rows]], gsend, grecv.at[i], dev)

    def forward(*names):
        for name in names:
            block_copy(name).start()

    def wait_rows(slot, *rows):
        for one in rows:
            i = arrives[slot, one]
            ref = xp.at[slot, k, spans[one]]
            remote(ref, ref, gsend, grecv.at[i], mate).wait_recv()

    def mate_copy(slot):
        return remote(xp.at[slot, k], xp.at[slot, k], msend, crecv.at[slot], mate)

    def wait_mate(slot):
        remote(xp.at[slot, 1 - k], xp.at[slot, 1 - k], msend, crecv.at[slot], mate).wait_recv()

    forward("e0h", "w0l", "s0l1", "s0h1", "e0l", "w0h", "s0l2", "s0h2")
    mate_copy(0).start()

    def hx_copy(i):
        to = rem(c + i, 16)
        return remote(hs.at[(2 * rem(to, 8) + to // 8) // 4], hx, hsend, hrecv, (r, to))

    copy_g.wait()
    copy_fs.wait()
    copy_hs.wait()
    gt[...] = gv[...].T
    racc[...] = jnp.zeros_like(racc)

    def z_dev(sign):
        return (r, yh * 8 + rem(z + sign + 8, 8))

    def message(s, m, sign):
        return remote(sb.at[s, m], rb.at[s, m], ssem, rsem.at[s, m], z_dev(sign))

    def chunk(s, offset):
        rows = pl.ds(pl.multiple_of(rem(z + offset + 8, 8) * 64, 64), 64)
        return pb[s, rows, :]

    def put(s, m, sign, value):
        sb[s, m] = encode(value)
        message(s, m, sign).start()

    def got(s, m):
        message(s, m, 1).wait_recv()
        return decode(rb[s, m])

    words = [sum((8 * kind + s) << (8 * i) for i, (kind, s) in enumerate(PLAN[at:at + 4])) for at in range(0, len(PLAN), 4)]

    def planned(t):
        word = jnp.int32(0)
        for i, value in enumerate(words):
            word = jnp.where(t // 4 == i, value, word)
        code = rem(lax.shift_right_logical(word, 8 * rem(t, 4)), 256)
        return code // 8, rem(code, 8)

    def slot_offset(p):
        dy = jnp.where(jnp.logical_or(p == 1, p >= 5), 1, 0)
        one = jnp.logical_or(p == 2, p == 5)
        three = jnp.logical_or(p == 3, p == 6)
        two = jnp.logical_or(p == 4, p == 7)
        dx = jnp.where(one, 1, 0) + jnp.where(two, 2, 0) + jnp.where(three, 3, 0)
        return dx, dy

    def half_copy(s, way, q):
        to = (r, q * 8 + rem(z + 9 - 2 * way, 8))
        return remote(hsb.at[s, 2 * way + q], hrb.at[s, 2 * way + yh], hssem, hrsem.at[s, 2 * way + yh], to)

    def y_copy(s):
        return remote(hsb.at[s, 4], hrb.at[s, 4], hssem, hrsem.at[s, 4], y_mate)

    def got_half(s, i):
        remote(hsb.at[s, i], hrb.at[s, i], hssem, hrsem.at[s, i], y_mate).wait_recv()
        return decode(hrb[s, i])

    def own_rows(s, q):
        return pb[s, pl.ds(pl.multiple_of(z * 64 + q * 32, 32), 32), :]

    def a_copy(s, kk, f):
        return remote(ga.at[s, kk], ar.at[r, 0:32], asend, arecv, (f, c))

    def p_copy(s, kk, f):
        return remote(pm.at[s, kk], ar.at[r, 32:40], psend, precv, (f, c))

    def mine(s, kk):
        return jnp.logical_and(s == 0, k == kk)

    def step(t, carry):
        kind, s = planned(t)

        @pl.when(kind == 0)
        def _():
            wait_mate(s)
            both = jnp.concatenate([xp[s, 0], xp[s, 1]], axis=1)
            pb[s] = jnp.dot(gt[...], both, preferred_element_type=jnp.float32)
            put(s, 0, 1 - 2 * rem(s, 2), chunk(s, 4))
            hsb[s, 4] = encode(own_rows(s, 1 - yh))
            y_copy(s).start()

        @pl.when(kind == 1)
        def _():
            for way, sign in ((0, 1), (1, -1)):
                long = rem(s, 2) == way

                @pl.when(long)
                def _():
                    put(s, 1 + way, sign, chunk(s, sign * 3) + got(s, 0))

                @pl.when(jnp.logical_not(long))
                def _():
                    put(s, 1 + way, sign, chunk(s, sign * 3))

        @pl.when(kind == 2)
        def _():
            for way, sign in ((0, 1), (1, -1)):
                put(s, 3 + way, sign, chunk(s, sign * 2) + got(s, 1 + way))

        @pl.when(kind == 3)
        def _():
            for way, sign in ((0, 1), (1, -1)):
                value = chunk(s, sign) + got(s, 3 + way)
                for q in (0, 1):
                    hsb[s, 2 * way + q] = encode(value[32 * q:32 * q + 32])
                    half_copy(s, way, q).start()

        @pl.when(kind == 4)
        def _():
            g = own_rows(s, yh)
            for i in (4, 0, 1, 2, 3):
                g = g + got_half(s, i)
            squares = g * g + 1e-30
            racc[...] += squares
            dx, dy = slot_offset(s)
            for kk in (0, 1):
                ga[s, kk] = g[:, kk * 128:(kk + 1) * 128]
                fsum[s, kk] = jnp.sum(squares[:, kk * 128:(kk + 1) * 128], axis=0, keepdims=True)

                @pl.when(mine(s, kk))
                def _():
                    ar[r, 0:32] = g[:, kk * 128:(kk + 1) * 128]

                @pl.when(jnp.logical_not(mine(s, kk)))
                def _():
                    a_copy(s, kk, row_of(dx, dy, kk)).start()

        @pl.when(kind == 6)
        def _():
            wait_rows(1, "l1", "h1")
            forward("e1l1", "w1h1")
            wait_rows(2, "l")
            forward("s2l")
            wait_rows(3, "h")
            forward("s3h")

        @pl.when(kind == 7)
        def _():
            wait_rows(1, "l2", "h2")
            forward("e1l2", "w1h2")
            wait_rows(3, "l")
            forward("e3l")
            wait_rows(2, "h")
            forward("w2h")
            for slot in (1, 2, 3):
                mate_copy(slot).start()

        @pl.when(kind == 10)
        def _():
            wait_rows(6, "l1", "l2")
            forward("e6l")
            wait_rows(5, "h1", "h2")
            forward("w5h")

        for slot, rows in ((4, ("l", "h")), (5, ("l",)), (6, ("h",)), (7, ("l", "h"))):
            @pl.when(jnp.logical_and(kind == 8, s == slot))
            def _():
                wait_rows(slot, *rows)
                mate_copy(slot).start()

        @pl.when(jnp.logical_and(kind == 9, diagonal))
        def _():
            hx[...] = hs[part // 4]
            for i in range(1, 16):
                hx_copy(i).start()

        return carry

    lax.fori_loop(0, len(PLAN), step, 0)

    @pl.when(jnp.logical_not(diagonal))
    def _():
        hx_copy(1).wait_recv()

    sums = jnp.sum(racc[...], axis=1, keepdims=True)
    lane = lax.broadcasted_iota(jnp.int32, (32, 128), 1)
    line = lax.broadcasted_iota(jnp.int32, (32, 128), 0)
    place = lane == line + rem(part, 4) * 32
    old = jnp.sum(jnp.where(place, hx[...], 0.0), axis=1, keepdims=True)
    hid = decay_rate * old + (1.0 - decay_rate) * (sums / feat_count)
    hid_row = jnp.sum(jnp.where(place, hid, 0.0), axis=0, keepdims=True)
    hid_sum = jnp.full((1, 128), jnp.sum(hid), jnp.float32)
    inverse = 1.0 / hid

    for s in range(PAIRS):
        for kk in (0, 1):
            weighted = jnp.sum(ga[s, kk] * ga[s, kk] * inverse, axis=0, keepdims=True)
            pm[s, kk] = jnp.concatenate([hid_row, fsum[s, kk], weighted, hid_sum, jnp.zeros((4, 128), jnp.float32)], axis=0)
            if s == 0:
                @pl.when(k == kk)
                def _():
                    ar[r, 32:40] = pm[s, kk]

                @pl.when(k != kk)
                def _():
                    p_copy(s, kk, row_of(*slot_offset(s), kk)).start()
            else:
                p_copy(s, kk, row_of(*slot_offset(s), kk)).start()

    def left(ref, sem):
        remote(ref, ref, sem, sem, mate).wait_send()

    def came(ref, sem):
        remote(ref, ref, sem, sem, mate).wait_recv()

    left(sb, ssem)
    left(hsb, hssem)
    left(xp.at[:, 0], msend)
    left(xp.at[0:7, 0], gsend)
    left(ar.at[0:15, 0:32], asend)
    came(cr.at[0:15], precv)
    cr[c] = jnp.sum(ar[:, 32:40], axis=0)

    def c_copy(i):
        return remote(cr.at[c], cr.at[c], csend, csrecv, (r, rem(c + i, 16)))

    for i in (8, 7, 9, 4, 12, 5, 11, 3, 13, 6, 10, 2, 14, 1, 15):
        c_copy(i).start()

    def b_copy(q):
        return remote(ar.at[q], tile.at[part], bsend, brecv, (r, q))

    came(ar.at[0:15, 0:32], arecv)
    tile[part] = ar[c]
    for i in range(1, 16):
        b_copy(rem(c + i, 16)).start()
    left(cr.at[0:15], psend)

    @pl.when(diagonal)
    def _():
        left(tr.at[0:15], hsend)

    came(cr.at[0:15], csrecv)
    both = jnp.sum(cr[...], axis=0)
    feat = decay_rate * fs[...] + (1.0 - decay_rate) * (both[1:2, :] / hid_count)
    feat_ref[...] = feat
    hid_mean = both[3:4, :] / hid_count
    tr[r] = jnp.full((1, 128), jnp.sum(both[2:3, :] / feat), jnp.float32)

    def t_copy(i):
        return remote(tr.at[r], tr.at[r], tsend, trecv, (rem(r + i, 16), c))

    for i in (12, 4, 8, 13, 14, 15, 9, 10, 11, 5, 6, 7, 3, 2, 1):
        t_copy(i).start()

    came(tile.at[0:15], brecv)
    left(cr.at[0:15], csend)
    left(ar.at[0:15], bsend)
    eye = lax.broadcasted_iota(jnp.int32, (128, 128), 0) == lax.broadcasted_iota(jnp.int32, (128, 128), 1)
    columns = []
    for q in range(4):
        line_q = tile[4 * q, 32:33] + tile[4 * q + 1, 32:33] + tile[4 * q + 2, 32:33] + tile[4 * q + 3, 32:33]
        hid_ref[q:q + 1, :] = line_q
        columns.append(lax.rsqrt(jnp.sum(jnp.where(eye, line_q, 0.0), axis=1, keepdims=True)))

    across0 = jnp.sqrt(hid_mean / feat)
    came(tr.at[0:15], trecv)
    mean = hid_mean * jnp.sum(tr[...], axis=0) / (hid_count * feat_count)
    rms = jnp.sqrt(mean)
    rms_ref[...] = rms
    across = across0 / jnp.maximum(1.0, rms)
    for q in range(4):
        g = tile[4 * q:4 * q + 4, 0:32].reshape(128, 128)
        upd_ref[128 * q:128 * q + 128, :] = g * columns[q] * across

    left(tr.at[0:15], tsend)


def writer(a, b, c, d, oa, ob, oc, od, sem):
    copies = [pltpu.make_async_copy(src, dst, sem.at[i]) for i, (src, dst) in enumerate(((a, oa), (b, ob), (c, oc), (d, od)))]
    for copy in copies:
        copy.start()
    for copy in copies:
        copy.wait()


def body(layer_input, grad_output, hid_state, feat_state):
    tokens = layer_input.shape[0]
    hid_count, feat_count = 8192.0, 2048.0
    vm = pl.BlockSpec(memory_space=pltpu.VMEM)
    hbm = pl.BlockSpec(memory_space=pl.ANY)
    f32, bf16 = jnp.float32, jnp.bfloat16
    dma = pltpu.SemaphoreType.DMA
    shapes = (
        jax.ShapeDtypeStruct((512, 128), f32),
        jax.ShapeDtypeStruct((4, 128), f32),
        jax.ShapeDtypeStruct((1, 128), f32),
        jax.ShapeDtypeStruct((1, 128), f32),
    )
    outs = pl.pallas_call(
        functools.partial(kernel, tokens, hid_count, feat_count),
        name="optimizer_step",
        out_shape=shapes,
        in_specs=[hbm, hbm, hbm, hbm],
        out_specs=(vm, vm, vm, vm),
        scratch_shapes=[
            pltpu.VMEM((4, 1, 128), f32),
            pltpu.VMEM((1, 128), f32),
            pltpu.VMEM((1, 128), f32),
            pltpu.VMEM((tokens, 512), bf16),
            pltpu.VMEM((512, tokens), bf16),
            pltpu.VMEM((PAIRS, 2, tokens, 128), bf16),
            pltpu.VMEM((PAIRS, 512, 256), f32),
            pltpu.VMEM((PAIRS, 5, TILE, 128), MSG),
            pltpu.VMEM((PAIRS, 5, TILE, 128), MSG),
            pltpu.VMEM((PAIRS, 5, HALF, 128), MSG),
            pltpu.VMEM((PAIRS, 5, HALF, 128), MSG),
            pltpu.VMEM((PAIRS, 2, 32, 128), f32),
            pltpu.VMEM((PAIRS, 2, 1, 128), f32),
            pltpu.VMEM((PAIRS, 2, 8, 128), f32),
            pltpu.VMEM((16, 40, 128), f32),
            pltpu.VMEM((16, 40, 128), f32),
            pltpu.VMEM((32, 256), f32),
            pltpu.VMEM((16, 8, 128), f32),
            pltpu.VMEM((16, 1, 128), f32),
            dma((4,)), dma, dma((18,)), dma, dma((PAIRS,)),
            dma, dma((PAIRS, 5)), dma, dma((PAIRS, 5)), dma, dma, dma, dma,
            dma, dma, dma, dma, dma, dma, dma, dma,
        ],
        compiler_params=pltpu.CompilerParams(
            collective_id=0, has_side_effects=True, vmem_limit_bytes=62 << 20
        ),
    )(layer_input, grad_output, hid_state.reshape(4, 1, 128), feat_state.reshape(1, 128))
    update, hid, feat, rms = pl.pallas_call(
        writer,
        name="write_results",
        out_shape=shapes,
        in_specs=[vm] * 4,
        out_specs=[hbm] * 4,
        scratch_shapes=[dma((4,))],
        compiler_params=pltpu.CompilerParams(vmem_limit_bytes=62 << 20),
    )(*outs)
    return update, hid.reshape(512), feat.reshape(128), rms[0, 0]


def solution(mesh):
    in_specs = (P("col", "row"), P("col", "row"), P("col"), P("row"))
    out_specs = (P("col", "row"), P("col"), P("row"), P())
    return jax.shard_map(body, mesh=mesh, in_specs=in_specs, out_specs=out_specs, check_vma=False)
```

time: 78.7 us -> 72.8 us (0.925)
  Pallas kernels: 77.9 us -> 72.1 us
    pallas_call x1, Pallas kernels: 76.2 us -> 70.4 us  [body(): pl.pallas_call(functools.partial(kernel, tokens, hid_count, feat_count),...]
where the time goes in v4:
time: 72.8 us; the launch traced here: 72.7 us
  Pallas kernels  72.1 us (99%)
    pallas_call x1, Pallas kernels, body(): pl.pallas_call(functools.partial(kernel, tokens, hid_count, feat_count),...  70.4 us
    pallas_call x1, Pallas kernels, body(): pl.pallas_call(writer, name='write_results', out_shape=shapes, in_specs=[...  1.7 us

profile of v4, /device:TPU:1, one launch (start us, length us, event | category | flops | bytes accessed | tf_op | source)
XLA Modules:
  0.0 72.7 jit_solution(9238523698366466102)
XLA Ops:
  0.6 70.4 %optimizer_step.1 = (f32[512,128]{1,0:T(8,128)}, f32[4,128]{1,0:T(4,128)}, f32[1,128]{1,0:T(1,128)}, f32[1,128]{1,0:T(1,128)}) custom-call(bf16[1536,128]{1,0:T(8,128)(2,1)} %x_hbm.1, bf16[1536,512]{1,0:T(8,128)(2,1)} %g_hbm.1, f32[4,1,128]{2,1,0:T(1,128)} %bitcast.6, f32[1,128]{1,0:T(1,128)} %bitcast.7), custom_call_target="tpu_custom_call" | custom-call | tf_op jit(solution)/shard_map/optimizer_step/pallas_call | solution.py:429
  71.0 1.7 %write_results.1 = (f32[512,128]{1,0:T(8,128)}, f32[4,128]{1,0:T(4,128)}, f32[1,128]{1,0:T(1,128)}, f32[1,128]{1,0:T(1,128)}) custom-call(f32[512,128]{1,0:T(8,128)} %get-tuple-element.12.a, f32[4,128]{1,0:T(4,128)} %get-tuple-element.13.b, f32[1,128]{1,0:T(1,128)} %get-tuple-element.14.c, f32[1,128]{1,0:T(1,128)} %get-tuple-element.15.d), custom_call_target="tpu_custom_call" | custom-call | tf_op jit(solution)/shard_map/write_results/pallas_call | solution.py:463

commit v5 on v4

--- a/solution.py
+++ b/solution.py
@@ -429,8 +429,8 @@
     outs = pl.pallas_call(
         functools.partial(kernel, tokens, hid_count, feat_count),
         name="optimizer_step",
-        out_shape=shapes,
-        in_specs=[hbm, hbm, hbm, hbm],
+        out_shape=tuple(pltpu.VMEM(one.shape, one.dtype) for one in shapes),
+        in_specs=[pl.BlockSpec(memory_space=pltpu.HBM)] * 4,
         out_specs=(vm, vm, vm, vm),
         scratch_shapes=[
             pltpu.VMEM((4, 1, 128), f32),
@@ -465,9 +465,9 @@
         name="write_results",
         out_shape=shapes,
         in_specs=[vm] * 4,
-        out_specs=[hbm] * 4,
+        out_specs=[pl.BlockSpec(memory_space=pltpu.HBM)] * 4,
         scratch_shapes=[dma((4,))],
-        compiler_params=pltpu.CompilerParams(vmem_limit_bytes=62 << 20),
+        compiler_params=pltpu.CompilerParams(vmem_limit_bytes=1 << 20),
     )(*outs)
     return update, hid.reshape(512), feat.reshape(128), rms[0, 0]
 

time: 72.8 us -> 71.1 us (0.977)
  Pallas kernels: 72.1 us -> 70.4 us
    pallas_call x1, Pallas kernels: 1.7 us -> 0.75 us  [body(): pl.pallas_call(writer, name='write_results', out_shape=shapes, in_specs=[...]
where the time goes in v5:
time: 71.1 us; the launch traced here: 71 us
  Pallas kernels  70.4 us (99%)
    pallas_call x1, Pallas kernels, body(): pl.pallas_call(functools.partial(kernel, tokens, hid_count, feat_count),...  69.6 us

profile of v5, /device:TPU:1, one launch (start us, length us, event | category | flops | bytes accessed | tf_op | source)
XLA Modules:
  0.0 71.0 jit_solution(10795107499529925854)
XLA Ops:
  0.6 69.6 %optimizer_step.1 = (f32[512,128]{1,0:T(8,128)S(1)}, f32[4,128]{1,0:T(4,128)S(1)}, f32[1,128]{1,0:T(1,128)S(1)}, f32[1,128]{1,0:T(1,128)S(1)}) custom-call(bf16[1536,128]{1,0:T(8,128)(2,1)} %x_hbm.1, bf16[1536,512]{1,0:T(8,128)(2,1)} %g_hbm.1, f32[4,1,128]{2,1,0:T(1,128)} %bitcast.6, f32[1,128]{1,0:T(1,128)} %bitcast.7), custom_call_target="tpu_custom_call" | custom-call | tf_op jit(solution)/shard_map/optimizer_step/pallas_call | solution.py:429
  70.3 0.7 %write_results.1 = (f32[512,128]{1,0:T(8,128)}, f32[4,128]{1,0:T(4,128)}, f32[1,128]{1,0:T(1,128)}, f32[1,128]{1,0:T(1,128)}) custom-call(f32[512,128]{1,0:T(8,128)S(1)} %get-tuple-element.12.a, f32[4,128]{1,0:T(4,128)S(1)} %get-tuple-element.13.b, f32[1,128]{1,0:T(1,128)S(1)} %get-tuple-element.14.c, f32[1,128]{1,0:T(1,128)S(1)} %get-tuple-element.15.d), custom_call_target="tpu_custom_call" | custom-call | tf_op jit(solution)/shard_map/write_results/pallas_call | solution.py:463

commit v6 on v5

--- a/solution.py
+++ b/solution.py
@@ -54,7 +54,7 @@
     tokens, hid_count, feat_count,
     x_hbm, g_hbm, hs_hbm, fs_hbm,
     upd_ref, hid_ref, feat_ref, rms_ref,
-    hs, hx, fs, gv, gt, xp, pb, sb, rb, hsb, hrb, ga, fsum, pm, ar, tile, racc, cr, tr,
+    hs, hx, fs, gv, gt, xp, pb, sb, rb, hsb, hrb, ga, fsum, pm, ar, tile, pr, cm, racc, cr, tr,
     lsem, gsend, grecv, msend, crecv, ssem, rsem, hssem, hrsem, asend, arecv, bsend, brecv,
     hsend, hrecv, psend, precv, csend, csrecv, tsend, trecv,
 ):
@@ -93,7 +93,7 @@
     down = (r, yh * 8 + rem(z + 7, 8))
     cross_up = (r, (1 - yh) * 8 + rem(z + 1, 8))
     cross_down = (r, (1 - yh) * 8 + rem(z + 7, 8))
-    peers = (east, west, side, mate, y_mate, up, down, cross_up, cross_down)
+    peers = (cross_up, cross_down, y_mate, east, west, side, up, down, mate)
     for dev in peers:
         pl.semaphore_signal(barrier, inc=1, device_id=dev, device_id_type=MESH)
     copy_x.wait()
@@ -198,10 +198,10 @@
         return pb[s, pl.ds(pl.multiple_of(z * 64 + q * 32, 32), 32), :]
 
     def a_copy(s, kk, f):
-        return remote(ga.at[s, kk], ar.at[r, 0:32], asend, arecv, (f, c))
+        return remote(ga.at[s, kk], ar.at[r], asend, arecv, (f, c))
 
     def p_copy(s, kk, f):
-        return remote(pm.at[s, kk], ar.at[r, 32:40], psend, precv, (f, c))
+        return remote(pm.at[s, kk], pr.at[r], psend, precv, (f, c))
 
     def mine(s, kk):
         return jnp.logical_and(s == 0, k == kk)
@@ -215,21 +215,22 @@
             both = jnp.concatenate([xp[s, 0], xp[s, 1]], axis=1)
             pb[s] = jnp.dot(gt[...], both, preferred_element_type=jnp.float32)
             put(s, 0, 1 - 2 * rem(s, 2), chunk(s, 4))
+
+        @pl.when(kind == 1)
+        def _():
+            for way, sign in ((0, 1), (1, -1)):
+                long = rem(s, 2) == way
+
+                @pl.when(long)
+                def _():
+                    put(s, 1 + way, sign, chunk(s, sign * 3) + got(s, 0))
+
+                @pl.when(jnp.logical_not(long))
+                def _():
+                    put(s, 1 + way, sign, chunk(s, sign * 3))
+
             hsb[s, 4] = encode(own_rows(s, 1 - yh))
             y_copy(s).start()
-
-        @pl.when(kind == 1)
-        def _():
-            for way, sign in ((0, 1), (1, -1)):
-                long = rem(s, 2) == way
-
-                @pl.when(long)
-                def _():
-                    put(s, 1 + way, sign, chunk(s, sign * 3) + got(s, 0))
-
-                @pl.when(jnp.logical_not(long))
-                def _():
-                    put(s, 1 + way, sign, chunk(s, sign * 3))
 
         @pl.when(kind == 2)
         def _():
@@ -258,7 +259,7 @@
 
                 @pl.when(mine(s, kk))
                 def _():
-                    ar[r, 0:32] = g[:, kk * 128:(kk + 1) * 128]
+                    ar[r] = g[:, kk * 128:(kk + 1) * 128]
 
                 @pl.when(jnp.logical_not(mine(s, kk)))
                 def _():
@@ -328,7 +329,7 @@
             if s == 0:
                 @pl.when(k == kk)
                 def _():
-                    ar[r, 32:40] = pm[s, kk]
+                    pr[r] = pm[s, kk]
 
                 @pl.when(k != kk)
                 def _():
@@ -346,12 +347,17 @@
     left(hsb, hssem)
     left(xp.at[:, 0], msend)
     left(xp.at[0:7, 0], gsend)
-    left(ar.at[0:15, 0:32], asend)
+    left(ar.at[0:15], asend)
     came(cr.at[0:15], precv)
-    cr[c] = jnp.sum(ar[:, 32:40], axis=0)
+    totals = jnp.sum(pr[...], axis=0)
+    top = lax.broadcasted_iota(jnp.int32, (8, 128), 0) == 0
+    for q in range(16):
+        cm[q] = jnp.where(top, pr[q], totals)
+    cr[part] = cm[c]
 
     def c_copy(i):
-        return remote(cr.at[c], cr.at[c], csend, csrecv, (r, rem(c + i, 16)))
+        q = rem(c + i, 16)
+        return remote(cm.at[q], cr.at[part], csend, csrecv, (r, q))
 
     for i in (8, 7, 9, 4, 12, 5, 11, 3, 13, 6, 10, 2, 14, 1, 15):
         c_copy(i).start()
@@ -359,7 +365,7 @@
     def b_copy(q):
         return remote(ar.at[q], tile.at[part], bsend, brecv, (r, q))
 
-    came(ar.at[0:15, 0:32], arecv)
+    came(ar.at[0:15], arecv)
     tile[part] = ar[c]
     for i in range(1, 16):
         b_copy(rem(c + i, 16)).start()
@@ -382,24 +388,24 @@
     for i in (12, 4, 8, 13, 14, 15, 9, 10, 11, 5, 6, 7, 3, 2, 1):
         t_copy(i).start()
 
+    eye = lax.broadcasted_iota(jnp.int32, (128, 128), 0) == lax.broadcasted_iota(jnp.int32, (128, 128), 1)
+    columns = []
+    for q in range(4):
+        line_q = cr[4 * q, 0:1] + cr[4 * q + 1, 0:1] + cr[4 * q + 2, 0:1] + cr[4 * q + 3, 0:1]
+        hid_ref[q:q + 1, :] = line_q
+        columns.append(lax.rsqrt(jnp.sum(jnp.where(eye, line_q, 0.0), axis=1, keepdims=True)))
+
+    across0 = jnp.sqrt(hid_mean / feat)
     came(tile.at[0:15], brecv)
     left(cr.at[0:15], csend)
     left(ar.at[0:15], bsend)
-    eye = lax.broadcasted_iota(jnp.int32, (128, 128), 0) == lax.broadcasted_iota(jnp.int32, (128, 128), 1)
-    columns = []
-    for q in range(4):
-        line_q = tile[4 * q, 32:33] + tile[4 * q + 1, 32:33] + tile[4 * q + 2, 32:33] + tile[4 * q + 3, 32:33]
-        hid_ref[q:q + 1, :] = line_q
-        columns.append(lax.rsqrt(jnp.sum(jnp.where(eye, line_q, 0.0), axis=1, keepdims=True)))
-
-    across0 = jnp.sqrt(hid_mean / feat)
     came(tr.at[0:15], trecv)
     mean = hid_mean * jnp.sum(tr[...], axis=0) / (hid_count * feat_count)
     rms = jnp.sqrt(mean)
     rms_ref[...] = rms
     across = across0 / jnp.maximum(1.0, rms)
     for q in range(4):
-        g = tile[4 * q:4 * q + 4, 0:32].reshape(128, 128)
+        g = tile[4 * q:4 * q + 4].reshape(128, 128)
         upd_ref[128 * q:128 * q + 128, :] = g * columns[q] * across
 
     left(tr.at[0:15], tsend)
@@ -447,8 +453,10 @@
             pltpu.VMEM((PAIRS, 2, 32, 128), f32),
             pltpu.VMEM((PAIRS, 2, 1, 128), f32),
             pltpu.VMEM((PAIRS, 2, 8, 128), f32),
-            pltpu.VMEM((16, 40, 128), f32),
-            pltpu.VMEM((16, 40, 128), f32),
+            pltpu.VMEM((16, 32, 128), f32),
+            pltpu.VMEM((16, 32, 128), f32),
+            pltpu.VMEM((16, 8, 128), f32),
+            pltpu.VMEM((16, 8, 128), f32),
             pltpu.VMEM((32, 256), f32),
             pltpu.VMEM((16, 8, 128), f32),
             pltpu.VMEM((16, 1, 128), f32),

time: 71.1 us -> 70.4 us (level)
  Pallas kernels: 70.4 us -> 69.6 us
    pallas_call x1, Pallas kernels: 69.6 us -> 68.9 us  [body(): pl.pallas_call(functools.partial(kernel, tokens, hid_count, feat_count),...]
where the time goes in v6:
time: 70.4 us; the launch traced here: 70.3 us
  Pallas kernels  69.6 us (99%)
    pallas_call x1, Pallas kernels, body(): pl.pallas_call(functools.partial(kernel, tokens, hid_count, feat_count),...  68.9 us

profile of v6, /device:TPU:1, one launch (start us, length us, event | category | flops | bytes accessed | tf_op | source)
XLA Modules:
  0.0 70.3 jit_solution(17715381875685545198)
XLA Ops:
  0.6 68.9 %optimizer_step.1 = (f32[512,128]{1,0:T(8,128)S(1)}, f32[4,128]{1,0:T(4,128)S(1)}, f32[1,128]{1,0:T(1,128)S(1)}, f32[1,128]{1,0:T(1,128)S(1)}) custom-call(bf16[1536,128]{1,0:T(8,128)(2,1)} %x_hbm.1, bf16[1536,512]{1,0:T(8,128)(2,1)} %g_hbm.1, f32[4,1,128]{2,1,0:T(1,128)} %bitcast.6, f32[1,128]{1,0:T(1,128)} %bitcast.7), custom_call_target="tpu_custom_call" | custom-call | tf_op jit(solution)/shard_map/optimizer_step/pallas_call | solution.py:435
  69.5 0.7 %write_results.1 = (f32[512,128]{1,0:T(8,128)}, f32[4,128]{1,0:T(4,128)}, f32[1,128]{1,0:T(1,128)}, f32[1,128]{1,0:T(1,128)}) custom-call(f32[512,128]{1,0:T(8,128)S(1)} %get-tuple-element.12.a, f32[4,128]{1,0:T(4,128)S(1)} %get-tuple-element.13.b, f32[1,128]{1,0:T(1,128)S(1)} %get-tuple-element.14.c, f32[1,128]{1,0:T(1,128)S(1)} %get-tuple-element.15.d), custom_call_target="tpu_custom_call" | custom-call | tf_op jit(solution)/shard_map/write_results/pallas_call | solution.py:471

commit v7 on v6

--- a/solution.py
+++ b/solution.py
@@ -25,7 +25,7 @@
 
 
 def rem(a, n):
-    return lax.rem(a, n)
+    return a % n if isinstance(a, int) else lax.rem(a, n)
 
 
 def encode(value):
@@ -166,15 +166,6 @@
         message(s, m, 1).wait_recv()
         return decode(rb[s, m])
 
-    words = [sum((8 * kind + s) << (8 * i) for i, (kind, s) in enumerate(PLAN[at:at + 4])) for at in range(0, len(PLAN), 4)]
-
-    def planned(t):
-        word = jnp.int32(0)
-        for i, value in enumerate(words):
-            word = jnp.where(t // 4 == i, value, word)
-        code = rem(lax.shift_right_logical(word, 8 * rem(t, 4)), 256)
-        return code // 8, rem(code, 8)
-
     def slot_offset(p):
         dy = jnp.where(jnp.logical_or(p == 1, p >= 5), 1, 0)
         one = jnp.logical_or(p == 2, p == 5)
@@ -206,8 +197,7 @@
     def mine(s, kk):
         return jnp.logical_and(s == 0, k == kk)
 
-    def step(t, carry):
-        kind, s = planned(t)
+    def step(kind, s):
 
         @pl.when(kind == 0)
         def _():
@@ -225,7 +215,7 @@
                 def _():
                     put(s, 1 + way, sign, chunk(s, sign * 3) + got(s, 0))
 
-                @pl.when(jnp.logical_not(long))
+                @pl.when(not long)
                 def _():
                     put(s, 1 + way, sign, chunk(s, sign * 3))
 
@@ -257,11 +247,11 @@
                 ga[s, kk] = g[:, kk * 128:(kk + 1) * 128]
                 fsum[s, kk] = jnp.sum(squares[:, kk * 128:(kk + 1) * 128], axis=0, keepdims=True)
 
-                @pl.when(mine(s, kk))
+                @pl.when(k == kk if s == 0 else False)
                 def _():
                     ar[r] = g[:, kk * 128:(kk + 1) * 128]
 
-                @pl.when(jnp.logical_not(mine(s, kk)))
+                @pl.when(k != kk if s == 0 else True)
                 def _():
                     a_copy(s, kk, row_of(dx, dy, kk)).start()
 
@@ -293,20 +283,19 @@
             forward("w5h")
 
         for slot, rows in ((4, ("l", "h")), (5, ("l",)), (6, ("h",)), (7, ("l", "h"))):
-            @pl.when(jnp.logical_and(kind == 8, s == slot))
+            @pl.when(kind == 8 and s == slot)
             def _():
                 wait_rows(slot, *rows)
                 mate_copy(slot).start()
 
-        @pl.when(jnp.logical_and(kind == 9, diagonal))
+        @pl.when(jnp.logical_and(kind == 9, diagonal) if kind == 9 else False)
         def _():
             hx[...] = hs[part // 4]
             for i in range(1, 16):
                 hx_copy(i).start()
 
-        return carry
-
-    lax.fori_loop(0, len(PLAN), step, 0)
+    for kind, s in PLAN:
+        step(kind, s)
 
     @pl.when(jnp.logical_not(diagonal))
     def _():

time: 70.4 us -> 70.5 us (level)
  no operation moved by 1% of the time
where the time goes in v7:
time: 70.5 us; the launch traced here: 70.4 us
  Pallas kernels  69.8 us (99%)
    pallas_call x1, Pallas kernels, body(): pl.pallas_call(functools.partial(kernel, tokens, hid_count, feat_count),...  69 us

profile of v7, /device:TPU:1, one launch (start us, length us, event | category | flops | bytes accessed | tf_op | source)
XLA Modules:
  0.0 70.4 jit_solution(17932536107134439998)
XLA Ops:
  0.6 69.0 %optimizer_step.1 = (f32[512,128]{1,0:T(8,128)S(1)}, f32[4,128]{1,0:T(4,128)S(1)}, f32[1,128]{1,0:T(1,128)S(1)}, f32[1,128]{1,0:T(1,128)S(1)}) custom-call(bf16[1536,128]{1,0:T(8,128)(2,1)} %x_hbm.1, bf16[1536,512]{1,0:T(8,128)(2,1)} %g_hbm.1, f32[4,1,128]{2,1,0:T(1,128)} %bitcast.6, f32[1,128]{1,0:T(1,128)} %bitcast.7), custom_call_target="tpu_custom_call" | custom-call | tf_op jit(solution)/shard_map/optimizer_step/pallas_call | solution.py:424
  69.6 0.7 %write_results.1 = (f32[512,128]{1,0:T(8,128)}, f32[4,128]{1,0:T(4,128)}, f32[1,128]{1,0:T(1,128)}, f32[1,128]{1,0:T(1,128)}) custom-call(f32[512,128]{1,0:T(8,128)S(1)} %get-tuple-element.12.a, f32[4,128]{1,0:T(4,128)S(1)} %get-tuple-element.13.b, f32[1,128]{1,0:T(1,128)S(1)} %get-tuple-element.14.c, f32[1,128]{1,0:T(1,128)S(1)} %get-tuple-element.15.d), custom_call_target="tpu_custom_call" | custom-call | tf_op jit(solution)/shard_map/write_results/pallas_call | solution.py:460
